TPU v7x, 32 devices: a whole 2x2x4 slice. The times are simulated.
32 devices in a mesh: chan: 2 (over y), dp: 16 (over z, x, core).
Axes of the slice: x: 2, y: 2, z: 4, core: 2. Of those that a mesh axis runs over, the one named last changes fastest.
Arguments:
- volume: bfloat16 [32, 32, 32, 256], P('dp', None, None, 'chan'), may hold values from -6 to 6
- filter_one: bfloat16 [3, 3, 3, 256, 256], P(None, None, None, 'chan'), may hold values from -0.078125 to 0.078125
- filter_two: bfloat16 [3, 3, 3, 256, 256], P(None, None, None, 'chan'), may hold values from -0.078125 to 0.078125
- cotangent: bfloat16 [32, 32, 32, 256], P('dp', None, None, 'chan'), may hold values from -6 to 6
Outputs:
- output: bfloat16 [32, 32, 32, 256], P('dp', None, None, 'chan')
- input_grad: bfloat16 [32, 32, 32, 256], P('dp', None, None, 'chan')
- grad_one: float32 [3, 3, 3, 256, 256], P(None, None, None, 'chan')
- grad_two: float32 [3, 3, 3, 256, 256], P(None, None, None, 'chan')
All inputs are finite; a program needn't handle non-finite values.
Results may differ from a plain program's by a relative error of at most 0.02525.
The roundings to bfloat16 on the way count: a program that leaves them out, or rounds other values in their place, can miss the bound.
Values may be sent and summed in bfloat16 or wider, within the bound.
No kernel may reach another device: no remote copies, remote signals or barrier semaphores. Data moves between devices by JAX's collectives and lax.ppermute only.
A program may use at most 128 MiB of HBM per device.

v0:
```python
import functools
import math

import jax
import jax.numpy as jnp
from jax import lax
from jax.experimental import pallas as pl
from jax.experimental.pallas import tpu as pltpu
from jax.sharding import PartitionSpec as P

VOX = 32
SLOPE = 0.3
HALF = 128
FULL = 256
TILE = 16
VMEM_LIMIT = 32 * 1024 * 1024


def extended(block, sides, width):
    for axis, dim in sides:
        count = lax.axis_size(axis)
        forward = [(i, i + 1) for i in range(count - 1)]
        forward.append((count - 1, 0))
        backward = [(target, source) for source, target in forward]
        low = lax.ppermute(
            lax.slice_in_dim(block, block.shape[dim] - width, None, axis=dim), axis, forward
        )
        high = lax.ppermute(lax.slice_in_dim(block, 0, width, axis=dim), axis, backward)
        block = jnp.concatenate([low, block, high], axis=dim)
    return block


def leaky(values):
    return jnp.where(values > 0, values, SLOPE * values)


def slope_of(values):
    return jnp.where(values > 0, jnp.float32(1.0), jnp.float32(SLOPE))


def tap_mask(rows, offset):
    base = lax.axis_index("dp") * rows
    total_rows = lax.axis_size("dp") * rows
    planes = jnp.mod(base + jnp.arange(rows, dtype=jnp.int32) - 1, total_rows)
    depth = jnp.mod(planes, VOX) + offset
    inside = jnp.logical_and(depth >= 0, depth < VOX)
    return inside[:, None, None, None]


def pad_plane(values):
    return jnp.pad(values, ((0, 0), (1, 1), (1, 1), (0, 0)))


def columns(plane, rows, height, breadth):
    taps = []
    for a in range(3):
        inside = tap_mask(rows, a - 1)
        depth_slab = plane[a : a + rows]
        depth_slab = jnp.where(inside, depth_slab, jnp.zeros_like(depth_slab))
        for b in range(3):
            for c in range(3):
                taps.append(depth_slab[:, b : b + height, c : c + breadth, :])
    stacked = jnp.concatenate(taps, axis=-1)
    return stacked.reshape(rows * height * breadth, stacked.shape[-1])


def plain(volume, filter_one, filter_two, cotangent):
    rows, height, breadth, narrow = volume.shape
    full = filter_one.shape[4]
    voxels = rows * height * breadth
    scale = 1.0 / math.sqrt(lax.axis_size("dp") * voxels)

    def forward(activity, weight):
        rim = extended(activity, (("dp", 0),), 1)
        plane = pad_plane(rim)
        stacked = columns(plane, rows, height, breadth)
        partial_value = jnp.dot(
            stacked, weight.reshape(27 * narrow, full), preferred_element_type=jnp.float32
        )
        summed = lax.psum_scatter(partial_value, "chan", scatter_dimension=1, tiled=True)
        return (plane, summed)

    def backward(plane, delta, weight):
        wide = lax.all_gather(delta, "chan", axis=3, tiled=True)
        rim = extended(wide, (("dp", 0),), 1)
        centre = rim[1 : rows + 1].reshape(voxels, full)
        stacked = columns(plane, rows, height, breadth)
        weight_grad = lax.dot_general(
            stacked, centre, (((0,), (0,)), ((), ())), preferred_element_type=jnp.float32
        )
        weight_grad = weight_grad.reshape(3, 3, 3, narrow, full)
        source = pad_plane(rim)
        total = jnp.zeros((rows, height, breadth, narrow), jnp.float32)
        for a in range(3):
            depth_slab = source[2 - a : 2 - a + rows]
            flat = depth_slab.reshape(-1, full)
            product = lax.dot_general(
                flat,
                weight[a].reshape(9 * narrow, full),
                (((1,), (1,)), ((), ())),
                preferred_element_type=jnp.float32,
            )
            product = product.reshape(rows, height + 2, breadth + 2, 9, narrow)
            part = jnp.zeros((rows, height, breadth, narrow), jnp.float32)
            for b in range(3):
                for c in range(3):
                    part = (
                        part
                        + product[:, 2 - b : 2 - b + height, 2 - c : 2 - c + breadth, b * 3 + c, :]
                    )
            inside = tap_mask(rows, 1 - a)
            total = total + jnp.where(inside, part, jnp.zeros_like(part))
        return (weight_grad, total.reshape(voxels, narrow))

    def layer_sum(weight_grad):
        return lax.psum(weight_grad, "dp")

    plane_one, pre_one = forward(volume, filter_one)
    act_one = leaky(pre_one).astype(jnp.bfloat16).reshape(rows, height, breadth, narrow)
    plane_two, pre_two = forward(act_one, filter_two)
    output = leaky(pre_two).astype(jnp.bfloat16).reshape(rows, height, breadth, narrow)
    delta_two = (cotangent.reshape(voxels, narrow).astype(jnp.float32) * slope_of(pre_two)).astype(
        jnp.bfloat16
    )
    local_two, back_two = backward(
        plane_two, delta_two.reshape(rows, height, breadth, narrow), filter_two
    )
    summed_two = layer_sum(local_two)
    delta_one = (back_two * slope_of(pre_one)).astype(jnp.bfloat16)
    local_one, back_one = backward(
        plane_one, delta_one.reshape(rows, height, breadth, narrow), filter_one
    )
    summed_one = layer_sum(local_one)
    input_grad = back_one.astype(jnp.bfloat16).reshape(rows, height, breadth, narrow)
    return (output, input_grad, summed_one * scale, summed_two * scale)


def is_seam():
    return lax.rem(lax.axis_index("dp") * 2, VOX) == 0


def place():
    at = lax.axis_index("dp")
    return at // 4, lax.rem(at // 2, 2), lax.rem(at, 2)


def shaped(values):
    return values.reshape(TILE, VOX, values.shape[1])


PARTS = {
    "all": dict(
        slots=((0, True), (1, True), (2, False), (1, False), (2, True), (3, True)),
        taps=(((0, 0), (1, 1), (2, 2)), ((0, 3), (1, 4), (2, 5))),
    ),
    "local": dict(
        slots=((0, True), (1, True), (0, False), (1, False)),
        taps=(((1, 0), (2, 3)), ((0, 2), (1, 1))),
    ),
    "rim": dict(
        slots=((0, True), (1, True)),
        taps=(((0, 0),), ((2, 1),)),
    ),
}


def filter_rows(kind):
    level, side, core = place()
    along, first = (side, 0) if kind == "quarters" else (lax.rem(level, 2), HALF)
    rows = [] if kind == "quarters" else [(HALF, 0)]
    if kind != "own":
        for unit in (core, 1 - core):
            rows += [(32, first + (2 * at + unit) * 32) for at in (along, 1 - along)]
    return rows


def copy_weights(kind, part, pieces, store, sems):
    me = lax.axis_index("chan")
    copies = []
    for (height, row), piece in zip(filter_rows(kind), pieces):
        if not isinstance(row, int):
            row = pl.multiple_of(row, 32)
        spans = ((0, 27),) if part != "rim" else ((0, 9), (18, 9))
        for side in range(2):
            column = pl.multiple_of((me if side == 0 else 1 - me) * HALF, HALF)
            for first, length in spans:
                taps = pl.ds(first, length)
                copies.append(
                    pltpu.make_async_copy(
                        piece.at[taps, :, pl.ds(column, HALF)],
                        store.at[taps, pl.ds(row, height), pl.ds(side * HALF, HALF)],
                        sems.at[len(copies)],
                    )
                )
    for copy in copies:
        copy.start()
    return copies


def fill_planes(part, planes, store):
    edge = jnp.zeros(store.shape[2:], store.dtype)
    seam = is_seam()
    for slot, (plane, always) in enumerate(PARTS[part]["slots"]):
        ref, at = planes[plane]
        store[slot, 0] = edge
        store[slot, VOX + 1] = edge
        if always:
            store[slot, 1 : VOX + 1] = ref[at]
            continue

        @pl.when(seam)
        def _():
            store[slot] = jnp.zeros(store.shape[1:], store.dtype)

        @pl.when(jnp.logical_not(seam))
        def _():
            store[slot, 1 : VOX + 1] = ref[at]


def conv_rows(store, weights, taps, row, flipped):
    pieces = []
    for _, slot in taps:
        for b in range(3):
            piece = store[slot, pl.ds(row + b, TILE)]
            pieces.append(piece.reshape(TILE * VOX, store.shape[3]))
    stacked = jnp.concatenate(pieces, axis=1)
    products = []
    for c in range(3):
        if flipped:
            tiles = [weights[(2 - a) * 9 + (2 - b) * 3 + 2 - c] for a, _ in taps for b in range(3)]
            dims = (((1,), (1,)), ((), ()))
            tiles = jnp.concatenate(tiles, axis=1)
        else:
            tiles = [weights[a * 9 + b * 3 + c] for a, _ in taps for b in range(3)]
            dims = (((1,), (0,)), ((), ()))
            tiles = jnp.concatenate(tiles, axis=0)
        products.append(
            lax.dot_general(stacked, tiles, dims, preferred_element_type=jnp.float32)
        )
    left, middle, right = products
    column = lax.rem(lax.broadcasted_iota(jnp.int32, left.shape, 0), VOX)
    left = jnp.where(column > 0, pltpu.roll(left, 1, 0), 0.0)
    right = jnp.where(column < VOX - 1, pltpu.roll(right, TILE * VOX - 1, 0), 0.0)
    return middle + left + right


def conv_kernel(part, kind, flipped, finish, counts, *refs):
    refs = list(refs)
    groups = []
    for count in counts:
        groups.append(refs[:count])
        refs = refs[count:]
    planes, pieces, begun, extra, outs = groups
    if kind == "ready":
        (weights,), copies = pieces, []
        (store,) = refs
    else:
        store, sems = refs
        weights = outs.pop()
        copies = copy_weights(kind, part, pieces, weights, sems)
    views = []
    for ref in planes:
        views += [(ref, at) for at in range(ref.shape[0])]
    fill_planes(part, views, store)
    for copy in copies:
        copy.wait()
    for plane in range(2):
        taps = PARTS[part]["taps"][plane]

        @pl.loop(0, VOX // TILE)
        def _(step):
            rows = pl.ds(pl.multiple_of(step * TILE, TILE), TILE)
            value = shaped(conv_rows(store, weights, taps, step * TILE, flipped))
            if begun:
                value = value + begun[0][plane, rows]
            finish(value, plane, rows, extra, outs)


def finish_partial(value, plane, rows, extra, outs):
    outs[0][plane, rows] = value


def finish_first(value, plane, rows, extra, outs):
    outs[plane][0, rows] = leaky(value).astype(jnp.bfloat16)


def finish_second(value, plane, rows, extra, outs):
    output, deltas = outs[0], outs[1:]
    output[plane, rows] = leaky(value[:, :, :HALF]).astype(jnp.bfloat16)
    slope = slope_of(value)
    for lane, cot in ((0, extra[0]), (HALF, extra[1])):
        delta = cot[plane, rows].astype(jnp.float32) * slope[:, :, lane : lane + HALF]
        deltas[plane][0, rows, :, lane : lane + HALF] = delta.astype(jnp.bfloat16)


def finish_back(value, plane, rows, extra, outs):
    act = extra[plane][0, rows].astype(jnp.float32)
    outs[plane][0, rows] = (value * slope_of(act)).astype(jnp.bfloat16)


def finish_last(value, plane, rows, extra, outs):
    outs[0][plane, rows] = value.astype(jnp.bfloat16)


def filter_kernel(low, mid_0, mid_1, high, delta_0, delta_1, keep, far, near, turned, moved):
    _, side, core = place()
    pixels = VOX * VOX
    seam = is_seam()
    sources = ((0, low), (1, mid_0), (2, mid_1), (3, high))
    for plane, ref in sources:
        flipped = ref[0].reshape(pixels, HALF).T
        for output_plane in range(2):
            tap = plane - output_plane
            if not 0 <= tap < 3:
                continue
            rows = slice(tap * HALF, (tap + 1) * HALF)
            columns = slice(output_plane * pixels, (output_plane + 1) * pixels)
            if plane in (1, 2) and tap != 1:
                turned[rows, columns] = jnp.where(seam, jnp.zeros_like(flipped), flipped)
            else:
                turned[rows, columns] = flipped
    for plane, ref in ((0, delta_0), (1, delta_1)):
        for c in range(3):
            moved[c, plane, 0] = jnp.zeros(moved.shape[3:], moved.dtype)
            moved[c, plane, VOX + 1] = jnp.zeros(moved.shape[3:], moved.dtype)
        moved[1, plane, 1 : VOX + 1] = ref[0]

        @pl.loop(0, VOX // TILE)
        def _(step):
            row = step * TILE
            values = ref[0, pl.ds(row, TILE)].reshape(TILE * VOX, FULL).astype(jnp.float32)
            column = lax.rem(lax.broadcasted_iota(jnp.int32, values.shape, 0), VOX)
            ahead = jnp.where(column < VOX - 1, pltpu.roll(values, TILE * VOX - 1, 0), 0.0)
            behind = jnp.where(column > 0, pltpu.roll(values, 1, 0), 0.0)
            moved[0, plane, pl.ds(row + 1, TILE)] = shaped(ahead.astype(jnp.bfloat16))
            moved[2, plane, pl.ds(row + 1, TILE)] = shaped(behind.astype(jnp.bfloat16))

    mine = lax.axis_index("chan") == core
    for b in range(3):

        @pl.loop(0, 3)
        def _(c):
            right = moved[c, :, 2 - b : 2 - b + VOX].reshape(2 * pixels, FULL)
            product = jnp.dot(turned[...], right, preferred_element_type=jnp.float32)
            kept = jnp.where(mine, product[:, :HALF], product[:, HALF:])
            sent = jnp.where(mine, product[:, HALF:], product[:, :HALF])
            for a in range(3):
                rows = slice(a * HALF, (a + 1) * HALF)
                tap = a * 9 + b * 3 + c
                keep[:, tap] = kept[rows].reshape(8, 16, HALF)
                blocks = sent[rows].reshape(2, 4, 16, HALF).astype(far.dtype)
                far[:, tap] = jnp.where(side == 0, blocks[1], blocks[0])
                near[:, tap] = jnp.where(side == 0, blocks[0], blocks[1])


def add_core_kernel(keep, far, near, kept, sent):
    _, side, _ = place()
    for target, came, first in ((kept, near, side * 4), (sent, far, (1 - side) * 4)):

        @pl.loop(0, 4)
        def _(block):
            total = keep[first + block] + came[block].astype(jnp.float32)
            target[block] = total.astype(target.dtype)


def add_side_kernel(keep, came, kept, *sent):
    level, _, _ = place()
    for step, target in enumerate((kept,) + sent):
        block = lax.rem(level + step, 4)
        total = keep[block] + came[block].astype(jnp.float32)
        target[...] = total.astype(target.dtype)


def add_level_kernel(scale, keep, *rest):
    total = keep[...]
    for came in rest[:-1]:
        total = total + came[...].astype(jnp.float32)
    rest[-1][...] = (total * scale).astype(rest[-1].dtype)


def add_core_level_kernel(keep, far, near, kept, *sent):
    level, side, _ = place()
    for step, target in enumerate((kept,) + sent):
        block = lax.rem(level + step, 4)
        for at, (came, first) in enumerate(((near, side * 4), (far, (1 - side) * 4))):
            total = keep[first + block] + came[block].astype(jnp.float32)
            target[at] = total.astype(target.dtype)


def add_level_far_kernel(keep, *rest):
    came, (near, far) = rest[:-2], rest[-2:]
    for at, target in ((0, near), (1, far)):
        total = keep[at]
        for block in came:
            total = total + block[at].astype(jnp.float32)
        target[...] = total.astype(target.dtype)


def join_level_kernel(own, *rest):
    level, _, _ = place()
    target = rest[-1]
    target[level] = own[...]
    for step, came in enumerate(rest[:-1], 1):
        target[lax.rem(level + 4 - step, 4)] = came[...]


def join_side_kernel(own, came, target):
    _, side, _ = place()
    target[pl.ds(side * 4, 4)] = own[...]
    target[pl.ds((1 - side) * 4, 4)] = came[...]


def join_core_kernel(own, came, grad):
    _, _, core = place()

    @pl.loop(0, 8)
    def _(block):
        row = pl.multiple_of(block * 16, 16)
        first = jnp.where(core == 0, own[block], came[block])
        second = jnp.where(core == 0, came[block], own[block])
        grad[:, pl.ds(row, 16), :HALF] = first.astype(jnp.float32)
        grad[:, pl.ds(row, 16), HALF:] = second.astype(jnp.float32)


WEIGHT = {"sum_two_core": 0, "sum_one_level": 10**10, "sum_one_levels": 10**10}


def hint(flops):
    return pl.CostEstimate(flops=flops, bytes_accessed=0, transcendentals=0)


def small_call(kernel, outs, operands, name):
    return pl.pallas_call(
        kernel,
        out_shape=[jax.ShapeDtypeStruct(shape, dtype) for shape, dtype in outs],
        in_specs=[pl.BlockSpec(memory_space=pltpu.VMEM)] * len(operands),
        out_specs=[pl.BlockSpec(memory_space=pltpu.VMEM)] * len(outs),
        compiler_params=pltpu.CompilerParams(vmem_limit_bytes=VMEM_LIMIT),
        cost_estimate=hint(WEIGHT.get(name, 3 * 10**9)),
        name=name,
    )(*operands)


PART = (27, 16, HALF)


def to_levels(blocks):
    count = lax.axis_size("dp")
    return [
        lax.ppermute(block, "dp", [(i, (i + 4 * step) % count) for i in range(count)])
        for step, block in enumerate(blocks, 1)
    ]


def sum_core(keep, far, near, name):
    outs = [((4,) + PART, jnp.float32), ((4,) + PART, jnp.bfloat16)]
    return small_call(add_core_kernel, outs, [keep, far, near], name + "_core")


def sum_side(keep, came, name):
    outs = [(PART, jnp.float32)] + [(PART, jnp.bfloat16)] * 3
    return small_call(add_side_kernel, outs, [keep, came], name + "_side")


def sum_level(keep, came, scale, name):
    kernel = functools.partial(add_level_kernel, scale)
    return small_call(kernel, [(PART, jnp.bfloat16)], [keep, *came], name + "_level")[0]


def sum_core_level(keep, far, near, name):
    pair = (2,) + PART
    outs = [(pair, jnp.float32)] + [(pair, jnp.bfloat16)] * 3
    return small_call(add_core_level_kernel, outs, [keep, far, near], name + "_core")


def sum_level_far(keep, came, name):
    outs = [(PART, jnp.float32), (PART, jnp.bfloat16)]
    return small_call(add_level_far_kernel, outs, [keep, *came], name + "_level")


def join_level(own, came, name):
    outs = [((4,) + PART, jnp.bfloat16)]
    return small_call(join_level_kernel, outs, [own, *came], name + "_levels")[0]


def join_side(own, came, name):
    outs = [((8,) + PART, jnp.bfloat16)]
    return small_call(join_side_kernel, outs, [own, came], name + "_sides")[0]


def join_core(own, came, name):
    outs = [((27, HALF, FULL), jnp.float32)]
    return small_call(join_core_kernel, outs, [own, came], name + "_cores")[0]


def conv_call(name, part, kind, finish, outs, planes, pieces, begun=(), extra=(), flipped=False):
    lanes = planes[0].shape[3]
    height = {"own": HALF, "quarters": HALF, "both": FULL, "ready": pieces[0].shape[1]}[kind]
    ready = kind == "ready"
    if not ready:
        outs = outs + [((27, height, FULL), jnp.bfloat16)]
    operands = [*planes, *pieces, *begun, *extra]
    counts = (len(planes), len(pieces), len(begun), len(extra), len(outs))
    specs = [pl.BlockSpec(memory_space=pltpu.VMEM) for _ in operands]
    if not ready:
        for at in range(len(planes), len(planes) + len(pieces)):
            own = kind != "quarters" and at == len(planes)
            specs[at] = pl.BlockSpec(memory_space=pltpu.HBM if own else pl.ANY)
    scratch = [pltpu.VMEM((len(PARTS[part]["slots"]), VOX + 2, VOX, lanes), jnp.bfloat16)]
    if not ready:
        scratch.append(pltpu.SemaphoreType.DMA((20,)))
    return pl.pallas_call(
        functools.partial(conv_kernel, part, kind, flipped, finish, counts),
        out_shape=[jax.ShapeDtypeStruct(shape, dtype) for shape, dtype in outs],
        in_specs=specs,
        out_specs=[pl.BlockSpec(memory_space=pltpu.VMEM)] * len(outs),
        scratch_shapes=scratch,
        compiler_params=pltpu.CompilerParams(vmem_limit_bytes=VMEM_LIMIT),
        cost_estimate=hint(0),
        name=name,
    )(*operands)


def filter_call(planes, mid_at, deltas, name):
    narrow = (1, VOX, VOX, HALF)
    specs = [
        pl.BlockSpec(narrow, functools.partial(lambda at, i: (at, 0, 0, 0), at)) for at in mid_at
    ]
    specs += [pl.BlockSpec((1, VOX, VOX, FULL), lambda i: (0, 0, 0, 0))] * 2
    return pl.pallas_call(
        filter_kernel,
        grid=(1,),
        out_shape=[
            jax.ShapeDtypeStruct((8, 27, 16, HALF), jnp.float32),
            jax.ShapeDtypeStruct((4, 27, 16, HALF), jnp.bfloat16),
            jax.ShapeDtypeStruct((4, 27, 16, HALF), jnp.bfloat16),
        ],
        in_specs=specs,
        out_specs=[
            pl.BlockSpec((size, 27, 16, HALF), lambda i: (0, 0, 0, 0)) for size in (8, 4, 4)
        ],
        scratch_shapes=[
            pltpu.VMEM((3 * HALF, 2 * VOX * VOX), jnp.bfloat16),
            pltpu.VMEM((3, 2, VOX + 2, VOX, FULL), jnp.bfloat16),
        ],
        compiler_params=pltpu.CompilerParams(vmem_limit_bytes=VMEM_LIMIT),
        cost_estimate=hint(0),
        name=name,
    )(*planes, *deltas)


def after(value, *earlier):
    return lax.optimization_barrier((value,) + earlier)[0]


def paired(volume, filter_one, filter_two, cotangent):
    count = lax.axis_size("dp")
    ahead = [(i, (i + 1) % count) for i in range(count)]
    behind = [(target, source) for source, target in ahead]
    scale = 1.0 / math.sqrt(count * 2 * VOX * VOX)
    one = filter_one.reshape(27, HALF, FULL)
    two = filter_two.reshape(27, HALF, FULL)
    level, side, core = place()

    def other(values):
        return lax.ppermute(values, "chan", [(0, 1), (1, 0)])

    def to_core(values):
        return lax.ppermute(values, "dp", [(i, i ^ 1) for i in range(count)])

    def to_side(values):
        return lax.ppermute(values, "dp", [(i, i ^ 2) for i in range(count)])

    def rims(first, last):
        return lax.ppermute(last, "dp", ahead), lax.ppermute(first, "dp", behind)

    wide = ((1, VOX, VOX, FULL), jnp.bfloat16)
    narrow = ((2, VOX, VOX, HALF), jnp.bfloat16)
    partial = ((2, VOX, VOX, FULL), jnp.float32)

    low_own, high_own = rims(volume[:1], volume[1:])
    one_0 = other(lax.dynamic_slice_in_dim(one, (2 * side + core) * 32, 32, axis=1))
    volume_other = other(after(volume, one_0, low_own, high_own))
    one_1 = to_side(one_0)
    one_2 = to_core(one_0)
    one_3 = to_core(one_1)
    quarters = [one_0, one_1, one_2, one_3]
    begun, own_ready = conv_call(
        "first_own", "all", "own", finish_partial, [partial],
        [after(low_own, volume_other), volume, high_own], [one],
    )
    two_0 = other(
        after(
            lax.dynamic_slice_in_dim(two, (2 * lax.rem(level, 2) + core) * 32, 32, axis=1),
            volume_other,
        )
    )
    low_other, high_other = rims(volume_other[:1], volume_other[1:])
    two_0 = after(two_0, begun)
    two_1 = lax.ppermute(two_0, "dp", [(i, i ^ 4) for i in range(count)])
    two_2 = to_core(two_0)
    cot_other = other(after(cotangent, two_0))
    begun, ready = conv_call(
        "first_other", "local", "quarters", finish_partial, [partial], [volume_other], quarters,
        [after(begun, two_0)],
    )
    act_0, act_1 = conv_call(
        "first_rim", "rim", "ready", finish_first, [wide, wide], [low_other, high_other],
        [ready], [begun],
    )
    low_act, high_act = rims(act_0, act_1)
    two_3 = to_core(two_1)
    pieces = [two, two_0, two_1, two_2, two_3]
    begun, ready = conv_call(
        "second_local", "local", "both", finish_partial, [partial], [act_0, act_1], pieces
    )
    output, delta_0, delta_1 = conv_call(
        "second_rim", "rim", "ready", finish_second, [narrow, wide, wide], [low_act, high_act],
        [ready], [begun], [cotangent, cot_other],
    )
    low_delta, high_delta = rims(delta_0, delta_1)
    keep, far, near = filter_call(
        [low_act, act_0, act_1, high_act], (0, 0, 0, 0), [delta_0, delta_1], "grad_two"
    )
    keep_two, *sends = sum_core_level(keep, to_core(far), to_core(near), "sum_two")
    levels_two = to_levels(sends)
    (begun,) = conv_call(
        "back_local", "local", "ready", finish_partial, [partial], [delta_0, after(delta_1, keep_two)],
        [ready], flipped=True,
    )
    prior_0, prior_1 = conv_call(
        "back_rim", "rim", "ready", finish_back, [wide, wide], [low_delta, high_delta],
        [ready], [begun], [act_0, act_1], flipped=True,
    )
    keep, far, near = filter_call(
        [low_own, volume, volume, high_own], (0, 0, 1, 0), [prior_0, prior_1], "grad_one"
    )
    far, near = to_core(far), to_core(near)
    keep_two, send_two = sum_level_far(after(keep_two, keep), levels_two, "sum_two")
    side_two = to_side(send_two)
    keep_one, send_one = sum_core(after(keep, keep_two), far, near, "sum_one")
    side_one = to_side(send_one)
    own_two = sum_level(after(keep_two, keep_one), [side_two], scale, "sum_two_side")
    levels_two = to_levels([own_two] * 3)
    keep_one, *sends = sum_side(after(keep_one, own_two), side_one, "sum_one")
    low_prior, high_prior = rims(after(prior_0, keep_one), after(prior_1, keep_one))
    levels_one = to_levels(sends)
    own_two = join_level(after(own_two, keep_one), levels_two, "sum_two")
    side_two = to_side(own_two)
    own_one = sum_level(after(keep_one, own_two), levels_one, scale, "sum_one")
    levels_one = to_levels([own_one] * 3)
    (input_grad,) = conv_call(
        "first_back", "all", "ready", finish_last, [narrow],
        [low_prior, after(prior_0, own_one), prior_1, high_prior], [own_ready], flipped=True,
    )
    own_two = join_side(after(own_two, input_grad), side_two, "sum_two")
    core_two = to_core(own_two)
    own_one = join_level(after(own_one, own_two), levels_one, "sum_one")
    side_one = to_side(own_one)
    summed_two = join_core(after(own_two, own_one), core_two, "sum_two")
    own_one = join_side(after(own_one, summed_two), side_one, "sum_one")
    summed_one = join_core(own_one, to_core(own_one), "sum_one")
    shape = filter_one.shape
    return output, input_grad, summed_one.reshape(shape), summed_two.reshape(shape)


def local(volume, filter_one, filter_two, cotangent):
    pair = lax.axis_size("chan") == 2 and lax.axis_size("dp") == 16
    if pair and volume.shape == (2, VOX, VOX, HALF):
        return paired(volume, filter_one, filter_two, cotangent)
    return plain(volume, filter_one, filter_two, cotangent)


def solution(mesh):
    in_specs = (
        P("dp", None, None, "chan"),
        P(None, None, None, "chan", None),
        P(None, None, None, "chan", None),
        P("dp", None, None, "chan"),
    )
    out_specs = (
        P("dp", None, None, "chan"),
        P("dp", None, None, "chan"),
        P(None, None, None, "chan", None),
        P(None, None, None, "chan", None),
    )
    return jax.shard_map(local, mesh=mesh, in_specs=in_specs, out_specs=out_specs, check_vma=False)
```

profile of v0, /device:TPU:0, one launch (start us, length us, event | category | flops | bytes accessed | tf_op | source)
XLA Modules:
  0.0 191.1 jit_solution(16993471171342314139)
XLA Ops:
  1.9 3.0 %collective-permute-start = (bf16[27,32,256]{2,1,0:T(8,128)(2,1)S(1)}, bf16[27,32,256]{2,1,0:T(8,128)(2,1)}, u32[]{:S(2)}, u32[]{:S(2)}) collective-permute-start(bf16[27,32,256]{2,1,0:T(8,128)(2,1)S(1)} %constant_dynamic-slice_fusion.1), channel_id=1, source_target_pairs={{0,16},{16,0},{1,17},{17,1},{2,18},{18,2},{3,19},{19,3},{4,20},{20... | collective-permute-start | bytes 1327112 | tf_op jit(solution)/shard_map/ppermute | solution.py:566
  6.1 4.4 %collective-permute-start.2 = (bf16[1,32,32,128]{3,2,1,0:T(8,128)(2,1)S(1)}, bf16[1,32,32,128]{3,2,1,0:T(8,128)(2,1)S(1)}, u32[]{:S(2)}, u32[]{:S(2)}) collective-permute-start(bf16[1,32,32,128]{3,2,1,0:T(8,128)(2,1)S(1)} %get-tuple-element.108), channel_id=1, source_target_pairs={{1,0},{2,1},{3,2},{4,3},{5,4},{6,5},{7,6},{8,7},{9,8},{10,9},{11,1... | collective-permute-start | bytes 786440 | tf_op jit(solution)/shard_map/ppermute | solution.py:575
  10.5 4.2 %collective-permute-done.1.refs_0_.low = bf16[1,32,32,128]{3,2,1,0:T(8,128)(2,1)S(1)} collective-permute-done((bf16[1,32,32,128]{3,2,1,0:T(8,128)(2,1)S(1)}, bf16[1,32,32,128]{3,2,1,0:T(8,128)(2,1)S(1)}, u32[]{:S(2)}, u32[]{:S(2)}) %collective-permute-start.1) | collective-permute-done | bytes 262176 | tf_op jit(solution)/shard_map/ppermute | solution.py:575
  19.5 10.4 %collective-permute-done.3.refs_0_ = bf16[2,32,32,128]{3,2,1,0:T(8,128)(2,1)S(1)} collective-permute-done((bf16[2,32,32,128]{3,2,1,0:T(8,128)(2,1)S(1)}, bf16[2,32,32,128]{3,2,1,0:T(8,128)(2,1)S(1)}, u32[]{:S(2)}, u32[]{:S(2)}) %collective-permute-start.3) | collective-permute-done | bytes 524320 | tf_op jit(solution)/shard_map/ppermute | solution.py:566
  31.4 5.4 %first_own.1 = (f32[2,32,32,256]{3,2,1,0:T(8,128)S(1)}, bf16[27,128,256]{2,1,0:T(8,128)(2,1)S(1)}) custom-call(bf16[1,32,32,128]{3,2,1,0:T(8,128)(2,1)S(1)} %collective-permute-done.1.refs_0_.low, bf16[2,32,32,128]{3,2,1,0:T(8,128)(2,1)S(1)} %copy-done, bf16[1,32,32,128]{3,2,1,0:T(8,128)(2,1)S(1)} %collective-permute-done.2.refs_2_.high, ...), custom_call_target="tpu_custom_call" | custom-call | tf_op jit(solution)/shard_map/first_own/pallas_call | solution.py:512
  36.8 5.3 %collective-permute-done.9.refs_3_ = bf16[27,32,256]{2,1,0:T(8,128)(2,1)S(1)} collective-permute-done((bf16[27,32,256]{2,1,0:T(8,128)(2,1)S(1)}, bf16[27,32,256]{2,1,0:T(8,128)(2,1)S(1)}, u32[]{:S(2)}, u32[]{:S(2)}) %collective-permute-start.9) | collective-permute-done | bytes 442400 | tf_op jit(solution)/shard_map/ppermute | solution.py:566
  42.4 4.4 %collective-permute-start.5 = (bf16[1,32,32,128]{3,2,1,0:T(8,128)(2,1)S(1)}, bf16[1,32,32,128]{3,2,1,0:T(8,128)(2,1)S(1)}, u32[]{:S(2)}, u32[]{:S(2)}) collective-permute-start(bf16[1,32,32,128]{3,2,1,0:T(8,128)(2,1)S(1)} %get-tuple-element.106), channel_id=1, source_target_pairs={{1,0},{2,1},{3,2},{4,3},{5,4},{6,5},{7,6},{8,7},{9,8},{10,9},{11,1... | collective-permute-start | bytes 786440 | tf_op jit(solution)/shard_map/ppermute | solution.py:575
  46.8 4.4 %first_other.1 = (f32[2,32,32,256]{3,2,1,0:T(8,128)S(1)}, bf16[27,128,256]{2,1,0:T(8,128)(2,1)S(1)}) custom-call(bf16[2,32,32,128]{3,2,1,0:T(8,128)(2,1)S(1)} %collective-permute-done.3.refs_0_, bf16[27,32,256]{2,1,0:T(8,128)(2,1)} %collective-permute-done.refs_1_, bf16[27,32,256]{2,1,0:T(8,128)(2,1)S(1)} %collective-permute-done.6.refs_2_, ...), custom_call_target="tpu_custom_call" | custom-call | tf_op jit(solution)/shard_map/first_other/pallas_call | solution.py:512
  51.2 2.9 %collective-permute-done.4.refs_0_ = bf16[1,32,32,128]{3,2,1,0:T(8,128)(2,1)S(1)} collective-permute-done((bf16[1,32,32,128]{3,2,1,0:T(8,128)(2,1)S(1)}, bf16[1,32,32,128]{3,2,1,0:T(8,128)(2,1)S(1)}, u32[]{:S(2)}, u32[]{:S(2)}) %collective-permute-start.4) | collective-permute-done | bytes 262176 | tf_op jit(solution)/shard_map/ppermute | solution.py:575
  56.6 4.7 %collective-permute-start.11 = (bf16[1,32,32,256]{3,2,1,0:T(8,128)(2,1)S(1)}, bf16[1,32,32,256]{3,2,1,0:T(8,128)(2,1)S(1)}, u32[]{:S(2)}, u32[]{:S(2)}) collective-permute-start(bf16[1,32,32,256]{3,2,1,0:T(8,128)(2,1)S(1)} %get-tuple-element.64.refs_0_.mid_0.refs_4_), channel_id=1, source_target_pairs={{1,0},{2,1},{3,2},{4,3},{5,4},{6,5},{7,6},{8,7},{9,8},{10,9},{11,1... | collective-permute-start | bytes 1572872 | tf_op jit(solution)/shard_map/ppermute | solution.py:575
  63.7 6.5 %second_local.1 = (f32[2,32,32,256]{3,2,1,0:T(8,128)S(1)}, bf16[27,256,256]{2,1,0:T(8,128)(2,1)S(1)}) custom-call(bf16[1,32,32,256]{3,2,1,0:T(8,128)(2,1)S(1)} %get-tuple-element.64.refs_0_.mid_0.refs_4_, bf16[1,32,32,256]{3,2,1,0:T(8,128)(2,1)S(1)} %get-tuple-element.63.refs_1_.mid_1.refs_5_, bf16[27,128,256]{2,1,0:T(8,128)(2,1)S(1)} %bitcast.5, ...), custom_call_target="tpu_custom_call" | custom-call | tf_op jit(solution)/shard_map/second_local/pallas_call | solution.py:512
  71.0 4.3 %second_rim.1 = (bf16[2,32,32,128]{3,2,1,0:T(8,128)(2,1)}, bf16[1,32,32,256]{3,2,1,0:T(8,128)(2,1)S(1)}, bf16[1,32,32,256]{3,2,1,0:T(8,128)(2,1)S(1)}) custom-call(bf16[1,32,32,256]{3,2,1,0:T(8,128)(2,1)S(1)} %collective-permute-done.10.refs_0_.low, bf16[1,32,32,256]{3,2,1,0:T(8,128)(2,1)S(1)} %collective-permute-done.11.refs_1_.high, ...), custom_call_target="tpu_custom_call" | custom-call | tf_op jit(solution)/shard_map/second_rim/pallas_call | solution.py:512
  79.7 6.2 %grad_two.1 = (f32[8,27,16,128]{3,2,1,0:T(8,128)S(1)}, bf16[4,27,16,128]{3,2,1,0:T(8,128)(2,1)S(1)}, bf16[4,27,16,128]{3,2,1,0:T(8,128)(2,1)S(1)}) custom-call(bf16[1,32,32,256]{3,2,1,0:T(8,128)(2,1)S(1)} %collective-permute-done.10.refs_0_.low, bf16[1,32,32,256]{3,2,1,0:T(8,128)(2,1)S(1)} %get-tuple-element.64.refs_0_.mid_0.refs_4_, ...), custom_call_target="tpu_custom_call" | custom-call | tf_op jit(solution)/shard_map/grad_two/pallas_call | solution.py:530
  92.5 5.8 %back_local.1.refs_3_ = f32[2,32,32,256]{3,2,1,0:T(8,128)S(1)} custom-call(bf16[1,32,32,256]{3,2,1,0:T(8,128)(2,1)S(1)} %get-tuple-element.70.delta_0.refs_0_, bf16[1,32,32,256]{3,2,1,0:T(8,128)(2,1)S(1)} %get-tuple-element.75.delta_1.refs_1_, bf16[27,256,256]{2,1,0:T(8,128)(2,1)S(1)} %get-tuple-element.65.refs_2_), custom_call_target="tpu_custom_call" | custom-call | tf_op jit(solution)/shard_map/back_local/pallas_call | solution.py:512
  98.3 3.4 %back_rim.1 = (bf16[1,32,32,256]{3,2,1,0:T(8,128)(2,1)S(1)}, bf16[1,32,32,256]{3,2,1,0:T(8,128)(2,1)S(1)}) custom-call(bf16[1,32,32,256]{3,2,1,0:T(8,128)(2,1)S(1)} %collective-permute-done.16.refs_0_, bf16[1,32,32,256]{3,2,1,0:T(8,128)(2,1)S(1)} %collective-permute-done.17.refs_1_, bf16[27,256,256]{2,1,0:T(8,128)(2,1)S(1)} %get-tuple-element.65.refs_2_, ...), custom_call_target="tpu_custom_call" | custom-call | tf_op jit(solution)/shard_map/back_rim/pallas_call | solution.py:512
  101.7 6.2 %grad_one.1 = (f32[8,27,16,128]{3,2,1,0:T(8,128)S(1)}, bf16[4,27,16,128]{3,2,1,0:T(8,128)(2,1)S(1)}, bf16[4,27,16,128]{3,2,1,0:T(8,128)(2,1)S(1)}) custom-call(bf16[1,32,32,128]{3,2,1,0:T(8,128)(2,1)S(1)} %collective-permute-done.1.refs_0_.low, bf16[2,32,32,128]{3,2,1,0:T(8,128)(2,1)S(1)} %copy-done, bf16[2,32,32,128]{3,2,1,0:T(8,128)(2,1)S(1)} %copy-done, ...), custom_call_target="tpu_custom_call" | custom-call | tf_op jit(solution)/shard_map/grad_one/pallas_call | solution.py:530
  112.7 12.6 %collective-permute-done.25.rest_0_ = bf16[27,16,128]{2,1,0:T(8,128)(2,1)S(1)} collective-permute-done((bf16[27,16,128]{2,1,0:T(8,128)(2,1)S(1)}, bf16[27,16,128]{2,1,0:T(8,128)(2,1)S(1)}, u32[]{:S(2)}, u32[]{:S(2)}) %collective-permute-start.25) | collective-permute-done | bytes 110624 | tf_op jit(solution)/shard_map/ppermute | solution.py:572
  134.3 5.2 %collective-permute-done.29.rest_1_ = bf16[27,16,128]{2,1,0:T(8,128)(2,1)S(1)} collective-permute-done((bf16[27,16,128]{2,1,0:T(8,128)(2,1)S(1)}, bf16[27,16,128]{2,1,0:T(8,128)(2,1)S(1)}, u32[]{:S(2)}, u32[]{:S(2)}) %collective-permute-start.29) | collective-permute-done | bytes 110624 | tf_op jit(solution)/shard_map/ppermute | solution.py:450
  140.8 5.0 %collective-permute-done.32.rest_1_ = bf16[27,16,128]{2,1,0:T(8,128)(2,1)S(1)} collective-permute-done((bf16[27,16,128]{2,1,0:T(8,128)(2,1)S(1)}, bf16[27,16,128]{2,1,0:T(8,128)(2,1)S(1)}, u32[]{:S(2)}, u32[]{:S(2)}) %collective-permute-start.32) | collective-permute-done | bytes 110624 | tf_op jit(solution)/shard_map/ppermute | solution.py:450
  145.9 6.7 %collective-permute-start.36 = (bf16[27,16,128]{2,1,0:T(8,128)(2,1)S(1)}, bf16[27,16,128]{2,1,0:T(8,128)(2,1)S(1)}, u32[]{:S(2)}, u32[]{:S(2)}) collective-permute-start(bf16[27,16,128]{2,1,0:T(8,128)(2,1)S(1)} %sum_one_level.1.own), channel_id=1, source_target_pairs={{0,4},{1,5},{2,6},{3,7},{4,8},{5,9},{6,10},{7,11},{8,12},{9,13},{1... | collective-permute-start | bytes 331784 | tf_op jit(solution)/shard_map/ppermute | solution.py:450
  152.5 3.4 %collective-permute-start.37 = (bf16[27,16,128]{2,1,0:T(8,128)(2,1)S(1)}, bf16[27,16,128]{2,1,0:T(8,128)(2,1)S(1)}, u32[]{:S(2)}, u32[]{:S(2)}) collective-permute-start(bf16[27,16,128]{2,1,0:T(8,128)(2,1)S(1)} %sum_one_level.1.own), channel_id=1, source_target_pairs={{0,8},{1,9},{2,10},{3,11},{4,12},{5,13},{6,14},{7,15},{8,0},{9,1},... | collective-permute-start | bytes 331784 | tf_op jit(solution)/shard_map/ppermute | solution.py:450
  156.6 9.2 %first_back.1 = bf16[2,32,32,128]{3,2,1,0:T(8,128)(2,1)} custom-call(bf16[1,32,32,256]{3,2,1,0:T(8,128)(2,1)S(1)} %collective-permute-done.27.refs_0_, bf16[1,32,32,256]{3,2,1,0:T(8,128)(2,1)S(1)} %get-tuple-element.100.delta_0.refs_1_, bf16[1,32,32,256]{3,2,1,0:T(8,128)(2,1)S(1)} %get-tuple-element.93.delta_1.refs_2_, ...), custom_call_target="tpu_custom_call" | custom-call | tf_op jit(solution)/shard_map/first_back/pallas_call | solution.py:512
  165.9 8.2 %collective-permute-start.39 = (bf16[8,27,16,128]{3,2,1,0:T(8,128)(2,1)S(1)}, bf16[8,27,16,128]{3,2,1,0:T(8,128)(2,1)S(1)}, u32[]{:S(2)}, u32[]{:S(2)}) collective-permute-start(bf16[8,27,16,128]{3,2,1,0:T(8,128)(2,1)S(1)} %sum_two_sides.1.own), channel_id=1, source_target_pairs={{0,1},{1,0},{2,3},{3,2},{4,5},{5,4},{6,7},{7,6},{8,9},{9,8},{10,11... | collective-permute-start | bytes 2654216 | tf_op jit(solution)/shard_map/ppermute | solution.py:569
  178.3 8.1 %collective-permute-done.40.came = bf16[4,27,16,128]{3,2,1,0:T(8,128)(2,1)S(1)} collective-permute-done((bf16[4,27,16,128]{3,2,1,0:T(8,128)(2,1)S(1)}, bf16[4,27,16,128]{3,2,1,0:T(8,128)(2,1)S(1)}, u32[]{:S(2)}, u32[]{:S(2)}) %collective-permute-start.40) | collective-permute-done | bytes 442400 | tf_op jit(solution)/shard_map/ppermute | solution.py:572
  (94 shorter events, 50.4 us)
Async XLA Ops:
  1.9 13.3 %collective-permute-start = (bf16[27,32,256]{2,1,0:T(8,128)(2,1)S(1)}, bf16[27,32,256]{2,1,0:T(8,128)(2,1)}, u32[]{:S(2)}, u32[]{:S(2)}) collective-permute-start(bf16[27,32,256]{2,1,0:T(8,128)(2,1)S(1)} %constant_dynamic-slice_fusion.1), channel_id=1, source_target_pairs={{0,16},{16,0},{1,17},{17,1},{2,18},{18,2},{3,19},{19,3},{4,20},{20... | collective-permute-start | bytes 1327112 | tf_op jit(solution)/shard_map/ppermute | solution.py:566
  15.2 14.7 %collective-permute-start.3 = (bf16[2,32,32,128]{3,2,1,0:T(8,128)(2,1)S(1)}, bf16[2,32,32,128]{3,2,1,0:T(8,128)(2,1)S(1)}, u32[]{:S(2)}, u32[]{:S(2)}) collective-permute-start(bf16[2,32,32,128]{3,2,1,0:T(8,128)(2,1)S(1)} %copy-done), channel_id=1, source_target_pairs={{0,16},{16,0},{1,17},{17,1},{2,18},{18,2},{3,19},{19,3},{4,20},{20... | collective-permute-start | bytes 1572872 | tf_op jit(solution)/shard_map/ppermute | solution.py:566
  16.9 14.0 %collective-permute-start.6 = (bf16[27,32,256]{2,1,0:T(8,128)(2,1)}, bf16[27,32,256]{2,1,0:T(8,128)(2,1)S(1)}, u32[]{:S(2)}, u32[]{:S(2)}) collective-permute-start(bf16[27,32,256]{2,1,0:T(8,128)(2,1)} %collective-permute-done.refs_1_), channel_id=1, source_target_pairs={{0,2},{1,3},{2,0},{3,1},{4,6},{5,7},{6,4},{7,5},{8,10},{9,11},{10,... | collective-permute-start | bytes 1327112 | tf_op jit(solution)/shard_map/ppermute | solution.py:572
  30.9 15.9 %collective-permute-start.7 = (bf16[27,32,256]{2,1,0:T(8,128)(2,1)}, bf16[27,32,256]{2,1,0:T(8,128)(2,1)S(1)}, u32[]{:S(2)}, u32[]{:S(2)}) collective-permute-start(bf16[27,32,256]{2,1,0:T(8,128)(2,1)} %collective-permute-done.refs_1_), channel_id=1, source_target_pairs={{0,1},{1,0},{2,3},{3,2},{4,5},{5,4},{6,7},{7,6},{8,9},{9,8},{10,11... | collective-permute-start | bytes 1327112 | tf_op jit(solution)/shard_map/ppermute | solution.py:569
  30.9 15.9 %collective-permute-start.8 = (bf16[27,32,256]{2,1,0:T(8,128)(2,1)S(1)}, bf16[27,32,256]{2,1,0:T(8,128)(2,1)S(1)}, u32[]{:S(2)}, u32[]{:S(2)}) collective-permute-start(bf16[27,32,256]{2,1,0:T(8,128)(2,1)S(1)} %collective-permute-done.6.refs_2_), channel_id=1, source_target_pairs={{0,1},{1,0},{2,3},{3,2},{4,5},{5,4},{6,7},{7,6},{8,9},{9,8},{10,11... | collective-permute-start | bytes 1327112 | tf_op jit(solution)/shard_map/ppermute | solution.py:569
  42.1 19.2 %collective-permute-start.12 = (bf16[27,32,256]{2,1,0:T(8,128)(2,1)S(1)}, bf16[27,32,256]{2,1,0:T(8,128)(2,1)S(1)}, u32[]{:S(2)}, u32[]{:S(2)}) collective-permute-start(bf16[27,32,256]{2,1,0:T(8,128)(2,1)S(1)} %collective-permute-done.9.refs_3_), channel_id=1, source_target_pairs={{0,4},{1,5},{2,6},{3,7},{4,0},{5,1},{6,2},{7,3},{8,12},{9,13},{10,... | collective-permute-start | bytes 1327112 | tf_op jit(solution)/shard_map/ppermute | solution.py:600
  56.6 13.7 %collective-permute-start.10 = (bf16[1,32,32,256]{3,2,1,0:T(8,128)(2,1)S(1)}, bf16[1,32,32,256]{3,2,1,0:T(8,128)(2,1)S(1)}, u32[]{:S(2)}, u32[]{:S(2)}) collective-permute-start(bf16[1,32,32,256]{3,2,1,0:T(8,128)(2,1)S(1)} %get-tuple-element.63.refs_1_.mid_1.refs_5_), channel_id=1, source_target_pairs={{0,1},{1,2},{2,3},{3,4},{4,5},{5,6},{6,7},{7,8},{8,9},{9,10},{10,1... | collective-permute-start | bytes 1572872 | tf_op jit(solution)/shard_map/ppermute | solution.py:575
  56.6 13.6 %collective-permute-start.11 = (bf16[1,32,32,256]{3,2,1,0:T(8,128)(2,1)S(1)}, bf16[1,32,32,256]{3,2,1,0:T(8,128)(2,1)S(1)}, u32[]{:S(2)}, u32[]{:S(2)}) collective-permute-start(bf16[1,32,32,256]{3,2,1,0:T(8,128)(2,1)S(1)} %get-tuple-element.64.refs_0_.mid_0.refs_4_), channel_id=1, source_target_pairs={{1,0},{2,1},{3,2},{4,3},{5,4},{6,5},{7,6},{8,7},{9,8},{10,9},{11,1... | collective-permute-start | bytes 1572872 | tf_op jit(solution)/shard_map/ppermute | solution.py:575
  75.3 23.0 %collective-permute-start.16 = (bf16[1,32,32,256]{3,2,1,0:T(8,128)(2,1)S(1)}, bf16[1,32,32,256]{3,2,1,0:T(8,128)(2,1)S(1)}, u32[]{:S(2)}, u32[]{:S(2)}) collective-permute-start(bf16[1,32,32,256]{3,2,1,0:T(8,128)(2,1)S(1)} %get-tuple-element.75.delta_1.refs_1_), channel_id=1, source_target_pairs={{0,1},{1,2},{2,3},{3,4},{4,5},{5,6},{6,7},{7,8},{8,9},{9,10},{10,1... | collective-permute-start | bytes 1572872 | tf_op jit(solution)/shard_map/ppermute | solution.py:575
  77.0 21.4 %collective-permute-start.17 = (bf16[1,32,32,256]{3,2,1,0:T(8,128)(2,1)S(1)}, bf16[1,32,32,256]{3,2,1,0:T(8,128)(2,1)S(1)}, u32[]{:S(2)}, u32[]{:S(2)}) collective-permute-start(bf16[1,32,32,256]{3,2,1,0:T(8,128)(2,1)S(1)} %get-tuple-element.70.delta_0.refs_0_), channel_id=1, source_target_pairs={{1,0},{2,1},{3,2},{4,3},{5,4},{6,5},{7,6},{8,7},{9,8},{10,9},{11,1... | collective-permute-start | bytes 1572872 | tf_op jit(solution)/shard_map/ppermute | solution.py:575
  88.6 19.9 %collective-permute-start.20 = (bf16[2,27,16,128]{3,2,1,0:T(8,128)(2,1)S(1)}, bf16[2,27,16,128]{3,2,1,0:T(8,128)(2,1)S(1)}, u32[]{:S(2)}, u32[]{:S(2)}) collective-permute-start(bf16[2,27,16,128]{3,2,1,0:T(8,128)(2,1)S(1)} %get-tuple-element.80), channel_id=1, source_target_pairs={{0,4},{1,5},{2,6},{3,7},{4,8},{5,9},{6,10},{7,11},{8,12},{9,13},{1... | collective-permute-start | bytes 663560 | tf_op jit(solution)/shard_map/ppermute | solution.py:450
  88.7 19.8 %collective-permute-start.21 = (bf16[2,27,16,128]{3,2,1,0:T(8,128)(2,1)S(1)}, bf16[2,27,16,128]{3,2,1,0:T(8,128)(2,1)S(1)}, u32[]{:S(2)}, u32[]{:S(2)}) collective-permute-start(bf16[2,27,16,128]{3,2,1,0:T(8,128)(2,1)S(1)} %get-tuple-element.81), channel_id=1, source_target_pairs={{0,8},{1,9},{2,10},{3,11},{4,12},{5,13},{6,14},{7,15},{8,0},{9,1},... | collective-permute-start | bytes 663560 | tf_op jit(solution)/shard_map/ppermute | solution.py:450
  90.1 18.4 %collective-permute-start.22 = (bf16[2,27,16,128]{3,2,1,0:T(8,128)(2,1)S(1)}, bf16[2,27,16,128]{3,2,1,0:T(8,128)(2,1)S(1)}, u32[]{:S(2)}, u32[]{:S(2)}) collective-permute-start(bf16[2,27,16,128]{3,2,1,0:T(8,128)(2,1)S(1)} %get-tuple-element.82), channel_id=1, source_target_pairs={{0,12},{1,13},{2,14},{3,15},{4,0},{5,1},{6,2},{7,3},{8,4},{9,5},{1... | collective-permute-start | bytes 663560 | tf_op jit(solution)/shard_map/ppermute | solution.py:450
  110.6 19.7 %collective-permute-start.26 = (bf16[4,27,16,128]{3,2,1,0:T(8,128)(2,1)S(1)}, bf16[4,27,16,128]{3,2,1,0:T(8,128)(2,1)S(1)}, u32[]{:S(2)}, u32[]{:S(2)}) collective-permute-start(bf16[4,27,16,128]{3,2,1,0:T(8,128)(2,1)S(1)} %get-tuple-element.91), channel_id=1, source_target_pairs={{0,2},{1,3},{2,0},{3,1},{4,6},{5,7},{6,4},{7,5},{8,10},{9,11},{10,... | collective-permute-start | bytes 1327112 | tf_op jit(solution)/shard_map/ppermute | solution.py:572
  111.4 13.9 %collective-permute-start.25 = (bf16[27,16,128]{2,1,0:T(8,128)(2,1)S(1)}, bf16[27,16,128]{2,1,0:T(8,128)(2,1)S(1)}, u32[]{:S(2)}, u32[]{:S(2)}) collective-permute-start(bf16[27,16,128]{2,1,0:T(8,128)(2,1)S(1)} %get-tuple-element.89), channel_id=1, source_target_pairs={{0,2},{1,3},{2,0},{3,1},{4,6},{5,7},{6,4},{7,5},{8,10},{9,11},{10,... | collective-permute-start | bytes 331784 | tf_op jit(solution)/shard_map/ppermute | solution.py:572
  126.2 13.3 %collective-permute-start.29 = (bf16[27,16,128]{2,1,0:T(8,128)(2,1)S(1)}, bf16[27,16,128]{2,1,0:T(8,128)(2,1)S(1)}, u32[]{:S(2)}, u32[]{:S(2)}) collective-permute-start(bf16[27,16,128]{2,1,0:T(8,128)(2,1)S(1)} %sum_two_side_level.1.own), channel_id=1, source_target_pairs={{0,8},{1,9},{2,10},{3,11},{4,12},{5,13},{6,14},{7,15},{8,0},{9,1},... | collective-permute-start | bytes 331784 | tf_op jit(solution)/shard_map/ppermute | solution.py:450
  130.5 15.3 %collective-permute-start.32 = (bf16[27,16,128]{2,1,0:T(8,128)(2,1)S(1)}, bf16[27,16,128]{2,1,0:T(8,128)(2,1)S(1)}, u32[]{:S(2)}, u32[]{:S(2)}) collective-permute-start(bf16[27,16,128]{2,1,0:T(8,128)(2,1)S(1)} %get-tuple-element.97), channel_id=1, source_target_pairs={{0,8},{1,9},{2,10},{3,11},{4,12},{5,13},{6,14},{7,15},{8,0},{9,1},... | collective-permute-start | bytes 331784 | tf_op jit(solution)/shard_map/ppermute | solution.py:450
  133.2 12.6 %collective-permute-start.33 = (bf16[27,16,128]{2,1,0:T(8,128)(2,1)S(1)}, bf16[27,16,128]{2,1,0:T(8,128)(2,1)S(1)}, u32[]{:S(2)}, u32[]{:S(2)}) collective-permute-start(bf16[27,16,128]{2,1,0:T(8,128)(2,1)S(1)} %get-tuple-element.98), channel_id=1, source_target_pairs={{0,12},{1,13},{2,14},{3,15},{4,0},{5,1},{6,2},{7,3},{8,4},{9,5},{1... | collective-permute-start | bytes 331784 | tf_op jit(solution)/shard_map/ppermute | solution.py:450
  139.5 26.3 %collective-permute-start.35 = (bf16[4,27,16,128]{3,2,1,0:T(8,128)(2,1)S(1)}, bf16[4,27,16,128]{3,2,1,0:T(8,128)(2,1)S(1)}, u32[]{:S(2)}, u32[]{:S(2)}) collective-permute-start(bf16[4,27,16,128]{3,2,1,0:T(8,128)(2,1)S(1)} %sum_two_levels.1.own), channel_id=1, source_target_pairs={{0,2},{1,3},{2,0},{3,1},{4,6},{5,7},{6,4},{7,5},{8,10},{9,11},{10,... | collective-permute-start | bytes 1327112 | tf_op jit(solution)/shard_map/ppermute | solution.py:572
  140.3 15.6 %collective-permute-start.34 = (bf16[1,32,32,256]{3,2,1,0:T(8,128)(2,1)S(1)}, bf16[1,32,32,256]{3,2,1,0:T(8,128)(2,1)S(1)}, u32[]{:S(2)}, u32[]{:S(2)}) collective-permute-start(bf16[1,32,32,256]{3,2,1,0:T(8,128)(2,1)S(1)} %get-tuple-element.100.delta_0.refs_1_), channel_id=1, source_target_pairs={{1,0},{2,1},{3,2},{4,3},{5,4},{6,5},{7,6},{8,7},{9,8},{10,9},{11,1... | collective-permute-start | bytes 1572872 | tf_op jit(solution)/shard_map/ppermute | solution.py:575
  140.3 16.3 %collective-permute-start.27 = (bf16[1,32,32,256]{3,2,1,0:T(8,128)(2,1)S(1)}, bf16[1,32,32,256]{3,2,1,0:T(8,128)(2,1)S(1)}, u32[]{:S(2)}, u32[]{:S(2)}) collective-permute-start(bf16[1,32,32,256]{3,2,1,0:T(8,128)(2,1)S(1)} %get-tuple-element.93.delta_1.refs_2_), channel_id=1, source_target_pairs={{0,1},{1,2},{2,3},{3,4},{4,5},{5,6},{6,7},{7,8},{8,9},{9,10},{10,1... | collective-permute-start | bytes 1572872 | tf_op jit(solution)/shard_map/ppermute | solution.py:575
  145.9 28.3 %collective-permute-start.36 = (bf16[27,16,128]{2,1,0:T(8,128)(2,1)S(1)}, bf16[27,16,128]{2,1,0:T(8,128)(2,1)S(1)}, u32[]{:S(2)}, u32[]{:S(2)}) collective-permute-start(bf16[27,16,128]{2,1,0:T(8,128)(2,1)S(1)} %sum_one_level.1.own), channel_id=1, source_target_pairs={{0,4},{1,5},{2,6},{3,7},{4,8},{5,9},{6,10},{7,11},{8,12},{9,13},{1... | collective-permute-start | bytes 331784 | tf_op jit(solution)/shard_map/ppermute | solution.py:450
  152.5 21.6 %collective-permute-start.37 = (bf16[27,16,128]{2,1,0:T(8,128)(2,1)S(1)}, bf16[27,16,128]{2,1,0:T(8,128)(2,1)S(1)}, u32[]{:S(2)}, u32[]{:S(2)}) collective-permute-start(bf16[27,16,128]{2,1,0:T(8,128)(2,1)S(1)} %sum_one_level.1.own), channel_id=1, source_target_pairs={{0,8},{1,9},{2,10},{3,11},{4,12},{5,13},{6,14},{7,15},{8,0},{9,1},... | collective-permute-start | bytes 331784 | tf_op jit(solution)/shard_map/ppermute | solution.py:450
  155.9 18.2 %collective-permute-start.38 = (bf16[27,16,128]{2,1,0:T(8,128)(2,1)S(1)}, bf16[27,16,128]{2,1,0:T(8,128)(2,1)S(1)}, u32[]{:S(2)}, u32[]{:S(2)}) collective-permute-start(bf16[27,16,128]{2,1,0:T(8,128)(2,1)S(1)} %sum_one_level.1.own), channel_id=1, source_target_pairs={{0,12},{1,13},{2,14},{3,15},{4,0},{5,1},{6,2},{7,3},{8,4},{9,5},{1... | collective-permute-start | bytes 331784 | tf_op jit(solution)/shard_map/ppermute | solution.py:450
  (22 other events, 192.3 us)
where the time goes:
time: 191 us
  waiting for transfers between devices  67.4 us (35%)
  starting transfers between devices  60.5 us (32%)
  Pallas kernels  58.9 us (31%)
  local copies, waits for them, and re-layouts  3.37 us (2%)
    pallas_call x8, Pallas kernels, conv_call(): pl.pallas_call(functools.partial(conv_kernel, part, kind, flipped, finish...  41.3 us
    ppermute x12, starting transfers between devices, to_levels(): lax.ppermute(block, 'dp', [(i, (i + 4 * step) % count) for i in range(cou...  21 us
    ppermute x5, waiting for transfers between devices, to_side(): return lax.ppermute(values, 'dp', [(i, i ^ 2) for i in range(count)])  20.6 us
    ppermute x10, starting transfers between devices, rims(): return (lax.ppermute(last, 'dp', ahead), lax.ppermute(first, 'dp', behind))  18.7 us
    ppermute x4, waiting for transfers between devices, other(): return lax.ppermute(values, 'chan', [(0, 1), (1, 0)])  17 us
    pallas_call x2, Pallas kernels, filter_call(): pl.pallas_call(filter_kernel, grid=(1,), out_shape=[jax.ShapeDtypeStruct(...  12.4 us
    ppermute x12, waiting for transfers between devices, to_levels(): lax.ppermute(block, 'dp', [(i, (i + 4 * step) % count) for i in range(cou...  12 us
    ppermute x10, starting transfers between devices, to_core(): return lax.ppermute(values, 'dp', [(i, i ^ 1) for i in range(count)])  10.4 us
  transfers between devices with their start and end apart: 42, of which 20 were waited for; matrix products, arithmetic and copies ran while one was open for 1% of the time, Pallas kernels for 27%

commit v1 on v0

--- a/solution.py
+++ b/solution.py
@@ -144,6 +144,11 @@
     return at // 4, lax.rem(at // 2, 2), lax.rem(at, 2)
 
 
+def place_bits():
+    level, side, _ = place()
+    return {"x": side, "z": lax.rem(level, 2), "zz": level // 2}
+
+
 def shaped(values):
     return values.reshape(TILE, VOX, values.shape[1])
 
@@ -302,8 +307,9 @@
     outs[0][plane, rows] = value.astype(jnp.bfloat16)
 
 
-def filter_kernel(low, mid_0, mid_1, high, delta_0, delta_1, keep, far, near, turned, moved):
-    _, side, core = place()
+def filter_kernel(axis, low, mid_0, mid_1, high, delta_0, delta_1, keep, far, near, turned, moved):
+    _, _, core = place()
+    bit = place_bits()[axis]
     pixels = VOX * VOX
     seam = is_seam()
     sources = ((0, low), (1, mid_0), (2, mid_1), (3, high))
@@ -349,13 +355,13 @@
                 tap = a * 9 + b * 3 + c
                 keep[:, tap] = kept[rows].reshape(8, 16, HALF)
                 blocks = sent[rows].reshape(2, 4, 16, HALF).astype(far.dtype)
-                far[:, tap] = jnp.where(side == 0, blocks[1], blocks[0])
-                near[:, tap] = jnp.where(side == 0, blocks[0], blocks[1])
-
-
-def add_core_kernel(keep, far, near, kept, sent):
-    _, side, _ = place()
-    for target, came, first in ((kept, near, side * 4), (sent, far, (1 - side) * 4)):
+                far[:, tap] = jnp.where(bit == 0, blocks[1], blocks[0])
+                near[:, tap] = jnp.where(bit == 0, blocks[0], blocks[1])
+
+
+def halve_core_kernel(axis, keep, far, near, kept, sent):
+    bit = place_bits()[axis]
+    for target, came, first in ((kept, near, bit * 4), (sent, far, (1 - bit) * 4)):
 
         @pl.loop(0, 4)
         def _(block):
@@ -363,66 +369,37 @@
             target[block] = total.astype(target.dtype)
 
 
-def add_side_kernel(keep, came, kept, *sent):
-    level, _, _ = place()
-    for step, target in enumerate((kept,) + sent):
-        block = lax.rem(level + step, 4)
-        total = keep[block] + came[block].astype(jnp.float32)
-        target[...] = total.astype(target.dtype)
-
-
-def add_level_kernel(scale, keep, *rest):
-    total = keep[...]
-    for came in rest[:-1]:
-        total = total + came[...].astype(jnp.float32)
-    rest[-1][...] = (total * scale).astype(rest[-1].dtype)
-
-
-def add_core_level_kernel(keep, far, near, kept, *sent):
-    level, side, _ = place()
-    for step, target in enumerate((kept,) + sent):
-        block = lax.rem(level + step, 4)
-        for at, (came, first) in enumerate(((near, side * 4), (far, (1 - side) * 4))):
-            total = keep[first + block] + came[block].astype(jnp.float32)
-            target[at] = total.astype(target.dtype)
-
-
-def add_level_far_kernel(keep, *rest):
-    came, (near, far) = rest[:-2], rest[-2:]
-    for at, target in ((0, near), (1, far)):
-        total = keep[at]
-        for block in came:
-            total = total + block[at].astype(jnp.float32)
-        target[...] = total.astype(target.dtype)
-
-
-def join_level_kernel(own, *rest):
-    level, _, _ = place()
-    target = rest[-1]
-    target[level] = own[...]
-    for step, came in enumerate(rest[:-1], 1):
-        target[lax.rem(level + 4 - step, 4)] = came[...]
-
-
-def join_side_kernel(own, came, target):
-    _, side, _ = place()
-    target[pl.ds(side * 4, 4)] = own[...]
-    target[pl.ds((1 - side) * 4, 4)] = came[...]
-
-
-def join_core_kernel(own, came, grad):
+def halve_kernel(axis, keep, came, kept, sent):
+    bit = place_bits()[axis]
+    half = keep.shape[0] // 2
+    for target, first in ((kept, bit * half), (sent, (1 - bit) * half)):
+        for block in range(half):
+            total = keep[first + block] + came[first + block].astype(jnp.float32)
+            target[block] = total.astype(target.dtype)
+
+
+def finish_kernel(scale, keep, came, total):
+    total[...] = ((keep[...] + came[...].astype(jnp.float32)) * scale).astype(total.dtype)
+
+
+def join_kernel(axis, own, came, target):
+    bit = place_bits()[axis]
+    half = own.shape[0]
+    target[pl.ds(bit * half, half)] = own[...]
+    target[pl.ds((1 - bit) * half, half)] = came[...]
+
+
+def join_core_kernel(order, own, came, grad):
     _, _, core = place()
-
-    @pl.loop(0, 8)
-    def _(block):
-        row = pl.multiple_of(block * 16, 16)
-        first = jnp.where(core == 0, own[block], came[block])
-        second = jnp.where(core == 0, came[block], own[block])
-        grad[:, pl.ds(row, 16), :HALF] = first.astype(jnp.float32)
-        grad[:, pl.ds(row, 16), HALF:] = second.astype(jnp.float32)
-
-
-WEIGHT = {"sum_two_core": 0, "sum_one_level": 10**10, "sum_one_levels": 10**10}
+    for at, block in enumerate(order):
+        rows = slice(block * 16, block * 16 + 16)
+        first = jnp.where(core == 0, own[at], came[at])
+        second = jnp.where(core == 0, came[at], own[at])
+        grad[:, rows, :HALF] = first.astype(jnp.float32)
+        grad[:, rows, HALF:] = second.astype(jnp.float32)
+
+
+WEIGHT = {"sum_two_core": 0, "first_rim": 3 * 10**9}
 
 
 def hint(flops):
@@ -444,53 +421,30 @@
 PART = (27, 16, HALF)
 
 
-def to_levels(blocks):
-    count = lax.axis_size("dp")
-    return [
-        lax.ppermute(block, "dp", [(i, (i + 4 * step) % count) for i in range(count)])
-        for step, block in enumerate(blocks, 1)
-    ]
-
-
-def sum_core(keep, far, near, name):
+def halve_core(axis, keep, far, near, name):
     outs = [((4,) + PART, jnp.float32), ((4,) + PART, jnp.bfloat16)]
-    return small_call(add_core_kernel, outs, [keep, far, near], name + "_core")
-
-
-def sum_side(keep, came, name):
-    outs = [(PART, jnp.float32)] + [(PART, jnp.bfloat16)] * 3
-    return small_call(add_side_kernel, outs, [keep, came], name + "_side")
-
-
-def sum_level(keep, came, scale, name):
-    kernel = functools.partial(add_level_kernel, scale)
-    return small_call(kernel, [(PART, jnp.bfloat16)], [keep, *came], name + "_level")[0]
-
-
-def sum_core_level(keep, far, near, name):
-    pair = (2,) + PART
-    outs = [(pair, jnp.float32)] + [(pair, jnp.bfloat16)] * 3
-    return small_call(add_core_level_kernel, outs, [keep, far, near], name + "_core")
-
-
-def sum_level_far(keep, came, name):
-    outs = [(PART, jnp.float32), (PART, jnp.bfloat16)]
-    return small_call(add_level_far_kernel, outs, [keep, *came], name + "_level")
-
-
-def join_level(own, came, name):
-    outs = [((4,) + PART, jnp.bfloat16)]
-    return small_call(join_level_kernel, outs, [own, *came], name + "_levels")[0]
-
-
-def join_side(own, came, name):
-    outs = [((8,) + PART, jnp.bfloat16)]
-    return small_call(join_side_kernel, outs, [own, came], name + "_sides")[0]
-
-
-def join_core(own, came, name):
+    return small_call(functools.partial(halve_core_kernel, axis), outs, [keep, far, near], name)
+
+
+def halve(axis, keep, came, name):
+    shape = (keep.shape[0] // 2,) + PART
+    outs = [(shape, jnp.float32), (shape, jnp.bfloat16)]
+    return small_call(functools.partial(halve_kernel, axis), outs, [keep, came], name)
+
+
+def finish(scale, keep, came, name):
+    outs = [((1,) + PART, jnp.bfloat16)]
+    return small_call(functools.partial(finish_kernel, scale), outs, [keep, came], name)[0]
+
+
+def join(axis, own, came, name):
+    outs = [((2 * own.shape[0],) + PART, jnp.bfloat16)]
+    return small_call(functools.partial(join_kernel, axis), outs, [own, came], name)[0]
+
+
+def join_core(order, own, came, name):
     outs = [((27, HALF, FULL), jnp.float32)]
-    return small_call(join_core_kernel, outs, [own, came], name + "_cores")[0]
+    return small_call(functools.partial(join_core_kernel, order), outs, [own, came], name)[0]
 
 
 def conv_call(name, part, kind, finish, outs, planes, pieces, begun=(), extra=(), flipped=False):
@@ -516,19 +470,19 @@
         out_specs=[pl.BlockSpec(memory_space=pltpu.VMEM)] * len(outs),
         scratch_shapes=scratch,
         compiler_params=pltpu.CompilerParams(vmem_limit_bytes=VMEM_LIMIT),
-        cost_estimate=hint(0),
+        cost_estimate=hint(WEIGHT.get(name, 0)),
         name=name,
     )(*operands)
 
 
-def filter_call(planes, mid_at, deltas, name):
+def filter_call(axis, planes, mid_at, deltas, name):
     narrow = (1, VOX, VOX, HALF)
     specs = [
         pl.BlockSpec(narrow, functools.partial(lambda at, i: (at, 0, 0, 0), at)) for at in mid_at
     ]
     specs += [pl.BlockSpec((1, VOX, VOX, FULL), lambda i: (0, 0, 0, 0))] * 2
     return pl.pallas_call(
-        filter_kernel,
+        functools.partial(filter_kernel, axis),
         grid=(1,),
         out_shape=[
             jax.ShapeDtypeStruct((8, 27, 16, HALF), jnp.float32),
@@ -571,6 +525,12 @@
     def to_side(values):
         return lax.ppermute(values, "dp", [(i, i ^ 2) for i in range(count)])
 
+    def to_level(values):
+        return lax.ppermute(values, "dp", [(i, i ^ 4) for i in range(count)])
+
+    def to_far_level(values):
+        return lax.ppermute(values, "dp", [(i, i ^ 8) for i in range(count)])
+
     def rims(first, last):
         return lax.ppermute(last, "dp", ahead), lax.ppermute(first, "dp", behind)
 
@@ -597,7 +557,7 @@
     )
     low_other, high_other = rims(volume_other[:1], volume_other[1:])
     two_0 = after(two_0, begun)
-    two_1 = lax.ppermute(two_0, "dp", [(i, i ^ 4) for i in range(count)])
+    two_1 = to_level(two_0)
     two_2 = to_core(two_0)
     cot_other = other(after(cotangent, two_0))
     begun, ready = conv_call(
@@ -620,46 +580,57 @@
     )
     low_delta, high_delta = rims(delta_0, delta_1)
     keep, far, near = filter_call(
-        [low_act, act_0, act_1, high_act], (0, 0, 0, 0), [delta_0, delta_1], "grad_two"
-    )
-    keep_two, *sends = sum_core_level(keep, to_core(far), to_core(near), "sum_two")
-    levels_two = to_levels(sends)
+        "z", [low_act, act_0, act_1, high_act], (0, 0, 0, 0), [delta_0, delta_1], "grad_two"
+    )
+    far, near = to_core(far), to_core(near)
     (begun,) = conv_call(
-        "back_local", "local", "ready", finish_partial, [partial], [delta_0, after(delta_1, keep_two)],
-        [ready], flipped=True,
-    )
+        "back_local", "local", "ready", finish_partial, [partial], [delta_0, delta_1], [ready],
+        flipped=True,
+    )
+    keep_two, sent = halve_core(
+        "z", after(keep, begun, low_delta, high_delta), far, near, "sum_two_core"
+    )
+    came_two = to_level(sent)
     prior_0, prior_1 = conv_call(
-        "back_rim", "rim", "ready", finish_back, [wide, wide], [low_delta, high_delta],
+        "back_rim", "rim", "ready", finish_back, [wide, wide], [after(low_delta, keep_two), high_delta],
         [ready], [begun], [act_0, act_1], flipped=True,
     )
     keep, far, near = filter_call(
-        [low_own, volume, volume, high_own], (0, 0, 1, 0), [prior_0, prior_1], "grad_one"
+        "x", [low_own, volume, volume, high_own], (0, 0, 1, 0), [prior_0, prior_1], "grad_one"
     )
     far, near = to_core(far), to_core(near)
-    keep_two, send_two = sum_level_far(after(keep_two, keep), levels_two, "sum_two")
-    side_two = to_side(send_two)
-    keep_one, send_one = sum_core(after(keep, keep_two), far, near, "sum_one")
-    side_one = to_side(send_one)
-    own_two = sum_level(after(keep_two, keep_one), [side_two], scale, "sum_two_side")
-    levels_two = to_levels([own_two] * 3)
-    keep_one, *sends = sum_side(after(keep_one, own_two), side_one, "sum_one")
+    keep_two, sent = halve("x", after(keep_two, keep), came_two, "sum_two_z")
+    came_two = to_side(sent)
+    keep_one, sent = halve_core("x", after(keep, keep_two), far, near, "sum_one_core")
+    came_one = to_side(sent)
+    keep_two, sent = halve("zz", after(keep_two, keep_one), came_two, "sum_two_x")
+    came_two = to_far_level(sent)
+    keep_one, sent = halve("z", after(keep_one, keep_two), came_one, "sum_one_x")
+    came_one = to_level(sent)
     low_prior, high_prior = rims(after(prior_0, keep_one), after(prior_1, keep_one))
-    levels_one = to_levels(sends)
-    own_two = join_level(after(own_two, keep_one), levels_two, "sum_two")
-    side_two = to_side(own_two)
-    own_one = sum_level(after(keep_one, own_two), levels_one, scale, "sum_one")
-    levels_one = to_levels([own_one] * 3)
+    own_two = finish(scale, after(keep_two, keep_one), came_two, "sum_two_zz")
+    came_two = to_far_level(own_two)
+    keep_one, sent = halve("zz", after(keep_one, own_two), came_one, "sum_one_z")
+    came_one = to_far_level(sent)
+    own_two = join("zz", after(own_two, keep_one), came_two, "join_two_zz")
+    came_two = to_level(own_two)
+    own_one = finish(scale, after(keep_one, own_two), came_one, "sum_one_zz")
+    came_one = to_far_level(own_one)
+    own_two = join("z", after(own_two, own_one), came_two, "join_two_z")
+    came_two = to_side(own_two)
+    own_one = join("zz", after(own_one, own_two, low_prior, high_prior), came_one, "join_one_zz")
+    came_one = to_level(own_one)
+    own_two = join("x", after(own_two, own_one), came_two, "join_two_x")
+    came_two = to_core(own_two)
+    own_one = join("z", after(own_one, own_two), came_one, "join_one_z")
+    came_one = to_side(own_one)
+    summed_two = join_core((0, 1, 4, 5, 2, 3, 6, 7), after(own_two, own_one), came_two, "grads_two")
     (input_grad,) = conv_call(
         "first_back", "all", "ready", finish_last, [narrow],
-        [low_prior, after(prior_0, own_one), prior_1, high_prior], [own_ready], flipped=True,
-    )
-    own_two = join_side(after(own_two, input_grad), side_two, "sum_two")
-    core_two = to_core(own_two)
-    own_one = join_level(after(own_one, own_two), levels_one, "sum_one")
-    side_one = to_side(own_one)
-    summed_two = join_core(after(own_two, own_one), core_two, "sum_two")
-    own_one = join_side(after(own_one, summed_two), side_one, "sum_one")
-    summed_one = join_core(own_one, to_core(own_one), "sum_one")
+        [low_prior, after(prior_0, summed_two), prior_1, high_prior], [own_ready], flipped=True,
+    )
+    own_one = join("x", after(own_one, input_grad), came_one, "join_one_x")
+    summed_one = join_core(tuple(range(8)), own_one, to_core(own_one), "grads_one")
     shape = filter_one.shape
     return output, input_grad, summed_one.reshape(shape), summed_two.reshape(shape)
 

time: 191 us -> 171 us (0.90)
  starting transfers between devices: 60.5 us -> 39.8 us
    ppermute x13 -> x9, waiting for transfers between devices: 12 us -> 28.3 us  [the longest x4 15.2 us: to_far_level(): return lax.ppermute(values, 'dp', [(i, i ^ 8) for i in range(count)])]
    ppermute x13 -> x9, starting transfers between devices: 21.2 us -> 7.66 us  [the longest x5 5.58 us: to_level(): return lax.ppermute(values, 'dp', [(i, i ^ 4) for i in range(count)])]
    ppermute x10, starting transfers between devices: 10.4 us -> 2.31 us  [to_core(): return lax.ppermute(values, 'dp', [(i, i ^ 1) for i in range(count)])]
    ppermute x4, waiting for transfers between devices: 17 us -> 10.5 us  [other(): return lax.ppermute(values, 'chan', [(0, 1), (1, 0)])]
    ppermute x10, waiting for transfers between devices: 9.92 us -> 4.34 us  [to_core(): return lax.ppermute(values, 'dp', [(i, i ^ 1) for i in range(count)])]
    ppermute x5, waiting for transfers between devices: 20.6 us -> 15.1 us  [to_side(): return lax.ppermute(values, 'dp', [(i, i ^ 2) for i in range(count)])]
    pallas_call x12 -> x16, Pallas kernels: 5.18 us -> 5.51 us  [small_call(): pl.pallas_call(kernel, out_shape=[jax.ShapeDtypeStruct(shape, dtype) for...]
  transfers between devices with their start and end apart: 42 -> 38, of which waited for: 20 -> 17; matrix products, arithmetic and copies ran while one was open for 1% -> 1% of each run, Pallas kernels for 27% -> 31%
where the time goes in v1:
time: 171 us; the launch traced here: 170 us
  waiting for transfers between devices  66.8 us (39%)
  Pallas kernels  59.4 us (35%)
  starting transfers between devices  39.8 us (23%)
  local copies, waits for them, and re-layouts  3.37 us (2%)
    pallas_call x8, Pallas kernels, conv_call(): pl.pallas_call(functools.partial(conv_kernel, part, kind, flipped, finish...  41.6 us
    ppermute x10, starting transfers between devices, rims(): return (lax.ppermute(last, 'dp', ahead), lax.ppermute(first, 'dp', behind))  20.3 us
    ppermute x4, waiting for transfers between devices, to_far_level(): return lax.ppermute(values, 'dp', [(i, i ^ 8) for i in range(count)])  15.2 us
    ppermute x5, waiting for transfers between devices, to_side(): return lax.ppermute(values, 'dp', [(i, i ^ 2) for i in range(count)])  15.1 us
    ppermute x5, waiting for transfers between devices, to_level(): return lax.ppermute(values, 'dp', [(i, i ^ 4) for i in range(count)])  13.1 us
    pallas_call x2, Pallas kernels, filter_call(): pl.pallas_call(functools.partial(filter_kernel, axis), grid=(1,), out_sha...  12.4 us
    ppermute x4, waiting for transfers between devices, other(): return lax.ppermute(values, 'chan', [(0, 1), (1, 0)])  10.5 us
    ppermute x10, waiting for transfers between devices, rims(): return (lax.ppermute(last, 'dp', ahead), lax.ppermute(first, 'dp', behind))  8.51 us
  transfers between devices with their start and end apart: 38, of which 17 were waited for; matrix products, arithmetic and copies ran while one was open for 1% of the time, Pallas kernels for 31%

profile of v1, /device:TPU:0, one launch (start us, length us, event | category | flops | bytes accessed | tf_op | source)
XLA Modules:
  0.0 170.4 jit_solution(16781995854263213569)
XLA Ops:
  1.9 3.0 %collective-permute-start = (bf16[27,32,256]{2,1,0:T(8,128)(2,1)S(1)}, bf16[27,32,256]{2,1,0:T(8,128)(2,1)}, u32[]{:S(2)}, u32[]{:S(2)}) collective-permute-start(bf16[27,32,256]{2,1,0:T(8,128)(2,1)S(1)} %constant_dynamic-slice_fusion.1), channel_id=1, source_target_pairs={{0,16},{16,0},{1,17},{17,1},{2,18},{18,2},{3,19},{19,3},{4,20},{20... | collective-permute-start | bytes 1327112 | tf_op jit(solution)/shard_map/ppermute | solution.py:520
  6.0 3.7 %collective-permute-start.2 = (bf16[1,32,32,128]{3,2,1,0:T(8,128)(2,1)S(1)}, bf16[1,32,32,128]{3,2,1,0:T(8,128)(2,1)S(1)}, u32[]{:S(2)}, u32[]{:S(2)}) collective-permute-start(bf16[1,32,32,128]{3,2,1,0:T(8,128)(2,1)S(1)} %get-tuple-element.118), channel_id=1, source_target_pairs={{1,0},{2,1},{3,2},{4,3},{5,4},{6,5},{7,6},{8,7},{9,8},{10,9},{11,1... | collective-permute-start | bytes 786440 | tf_op jit(solution)/shard_map/ppermute | solution.py:535
  9.7 3.9 %collective-permute-done.2.refs_2_.high = bf16[1,32,32,128]{3,2,1,0:T(8,128)(2,1)S(1)} collective-permute-done((bf16[1,32,32,128]{3,2,1,0:T(8,128)(2,1)S(1)}, bf16[1,32,32,128]{3,2,1,0:T(8,128)(2,1)S(1)}, u32[]{:S(2)}, u32[]{:S(2)}) %collective-permute-start.2) | collective-permute-done | bytes 262176 | tf_op jit(solution)/shard_map/ppermute | solution.py:535
  13.6 4.6 %collective-permute-done.1.refs_0_.low = bf16[1,32,32,128]{3,2,1,0:T(8,128)(2,1)S(1)} collective-permute-done((bf16[1,32,32,128]{3,2,1,0:T(8,128)(2,1)S(1)}, bf16[1,32,32,128]{3,2,1,0:T(8,128)(2,1)S(1)}, u32[]{:S(2)}, u32[]{:S(2)}) %collective-permute-start.1) | collective-permute-done | bytes 262176 | tf_op jit(solution)/shard_map/ppermute | solution.py:535
  19.8 9.8 %collective-permute-done.3.refs_0_ = bf16[2,32,32,128]{3,2,1,0:T(8,128)(2,1)S(1)} collective-permute-done((bf16[2,32,32,128]{3,2,1,0:T(8,128)(2,1)S(1)}, bf16[2,32,32,128]{3,2,1,0:T(8,128)(2,1)S(1)}, u32[]{:S(2)}, u32[]{:S(2)}) %collective-permute-start.3) | collective-permute-done | bytes 524320 | tf_op jit(solution)/shard_map/ppermute | solution.py:520
  31.3 3.2 %collective-permute-start.5 = (bf16[1,32,32,128]{3,2,1,0:T(8,128)(2,1)S(1)}, bf16[1,32,32,128]{3,2,1,0:T(8,128)(2,1)S(1)}, u32[]{:S(2)}, u32[]{:S(2)}) collective-permute-start(bf16[1,32,32,128]{3,2,1,0:T(8,128)(2,1)S(1)} %get-tuple-element.116), channel_id=1, source_target_pairs={{1,0},{2,1},{3,2},{4,3},{5,4},{6,5},{7,6},{8,7},{9,8},{10,9},{11,1... | collective-permute-start | bytes 786440 | tf_op jit(solution)/shard_map/ppermute | solution.py:535
  34.5 5.4 %first_own.1 = (f32[2,32,32,256]{3,2,1,0:T(8,128)S(1)}, bf16[27,128,256]{2,1,0:T(8,128)(2,1)S(1)}) custom-call(bf16[1,32,32,128]{3,2,1,0:T(8,128)(2,1)S(1)} %collective-permute-done.1.refs_0_.low, bf16[2,32,32,128]{3,2,1,0:T(8,128)(2,1)S(1)} %copy-done, bf16[1,32,32,128]{3,2,1,0:T(8,128)(2,1)S(1)} %collective-permute-done.2.refs_2_.high, ...), custom_call_target="tpu_custom_call" | custom-call | tf_op jit(solution)/shard_map/first_own/pallas_call | solution.py:466
  41.2 4.6 %first_other.1 = (f32[2,32,32,256]{3,2,1,0:T(8,128)S(1)}, bf16[27,128,256]{2,1,0:T(8,128)(2,1)S(1)}) custom-call(bf16[2,32,32,128]{3,2,1,0:T(8,128)(2,1)S(1)} %collective-permute-done.3.refs_0_, bf16[27,32,256]{2,1,0:T(8,128)(2,1)} %collective-permute-done.refs_1_, bf16[27,32,256]{2,1,0:T(8,128)(2,1)} %collective-permute-done.6.refs_2_, ...), custom_call_target="tpu_custom_call" | custom-call | tf_op jit(solution)/shard_map/first_other/pallas_call | solution.py:466
  48.4 4.4 %collective-permute-start.11 = (bf16[1,32,32,256]{3,2,1,0:T(8,128)(2,1)S(1)}, bf16[1,32,32,256]{3,2,1,0:T(8,128)(2,1)S(1)}, u32[]{:S(2)}, u32[]{:S(2)}) collective-permute-start(bf16[1,32,32,256]{3,2,1,0:T(8,128)(2,1)S(1)} %get-tuple-element.69.refs_0_.mid_0.refs_4_), channel_id=1, source_target_pairs={{1,0},{2,1},{3,2},{4,3},{5,4},{6,5},{7,6},{8,7},{9,8},{10,9},{11,1... | collective-permute-start | bytes 1572872 | tf_op jit(solution)/shard_map/ppermute | solution.py:535
  55.5 6.5 %second_local.1 = (f32[2,32,32,256]{3,2,1,0:T(8,128)S(1)}, bf16[27,256,256]{2,1,0:T(8,128)(2,1)S(1)}) custom-call(bf16[1,32,32,256]{3,2,1,0:T(8,128)(2,1)S(1)} %get-tuple-element.69.refs_0_.mid_0.refs_4_, bf16[1,32,32,256]{3,2,1,0:T(8,128)(2,1)S(1)} %get-tuple-element.68.refs_1_.mid_1.refs_5_, bf16[27,128,256]{2,1,0:T(8,128)(2,1)S(1)} %bitcast.5, ...), custom_call_target="tpu_custom_call" | custom-call | tf_op jit(solution)/shard_map/second_local/pallas_call | solution.py:466
  62.7 4.3 %second_rim.1 = (bf16[2,32,32,128]{3,2,1,0:T(8,128)(2,1)}, bf16[1,32,32,256]{3,2,1,0:T(8,128)(2,1)S(1)}, bf16[1,32,32,256]{3,2,1,0:T(8,128)(2,1)S(1)}) custom-call(bf16[1,32,32,256]{3,2,1,0:T(8,128)(2,1)S(1)} %collective-permute-done.10.refs_0_.low, bf16[1,32,32,256]{3,2,1,0:T(8,128)(2,1)S(1)} %collective-permute-done.11.refs_1_.high, ...), custom_call_target="tpu_custom_call" | custom-call | tf_op jit(solution)/shard_map/second_rim/pallas_call | solution.py:466
  67.2 4.2 %collective-permute-start.17 = (bf16[1,32,32,256]{3,2,1,0:T(8,128)(2,1)S(1)}, bf16[1,32,32,256]{3,2,1,0:T(8,128)(2,1)S(1)}, u32[]{:S(2)}, u32[]{:S(2)}) collective-permute-start(bf16[1,32,32,256]{3,2,1,0:T(8,128)(2,1)S(1)} %get-tuple-element.75.delta_0.refs_0_), channel_id=1, source_target_pairs={{1,0},{2,1},{3,2},{4,3},{5,4},{6,5},{7,6},{8,7},{9,8},{10,9},{11,1... | collective-permute-start | bytes 1572872 | tf_op jit(solution)/shard_map/ppermute | solution.py:535
  71.5 6.2 %grad_two.1 = (f32[8,27,16,128]{3,2,1,0:T(8,128)S(1)}, bf16[4,27,16,128]{3,2,1,0:T(8,128)(2,1)S(1)}, bf16[4,27,16,128]{3,2,1,0:T(8,128)(2,1)S(1)}) custom-call(bf16[1,32,32,256]{3,2,1,0:T(8,128)(2,1)S(1)} %collective-permute-done.10.refs_0_.low, bf16[1,32,32,256]{3,2,1,0:T(8,128)(2,1)S(1)} %get-tuple-element.69.refs_0_.mid_0.refs_4_, ...), custom_call_target="tpu_custom_call" | custom-call | tf_op jit(solution)/shard_map/grad_two/pallas_call | solution.py:484
  78.2 5.8 %back_local.1.refs_3_ = f32[2,32,32,256]{3,2,1,0:T(8,128)S(1)} custom-call(bf16[1,32,32,256]{3,2,1,0:T(8,128)(2,1)S(1)} %get-tuple-element.75.delta_0.refs_0_, bf16[1,32,32,256]{3,2,1,0:T(8,128)(2,1)S(1)} %get-tuple-element.74.delta_1.refs_1_, bf16[27,256,256]{2,1,0:T(8,128)(2,1)S(1)} %get-tuple-element.70.refs_2_), custom_call_target="tpu_custom_call" | custom-call | tf_op jit(solution)/shard_map/back_local/pallas_call | solution.py:466
  84.4 3.4 %back_rim.1 = (bf16[1,32,32,256]{3,2,1,0:T(8,128)(2,1)S(1)}, bf16[1,32,32,256]{3,2,1,0:T(8,128)(2,1)S(1)}) custom-call(bf16[1,32,32,256]{3,2,1,0:T(8,128)(2,1)S(1)} %collective-permute-done.16.refs_0_, bf16[1,32,32,256]{3,2,1,0:T(8,128)(2,1)S(1)} %collective-permute-done.17.refs_1_, bf16[27,256,256]{2,1,0:T(8,128)(2,1)S(1)} %get-tuple-element.70.refs_2_, ...), custom_call_target="tpu_custom_call" | custom-call | tf_op jit(solution)/shard_map/back_rim/pallas_call | solution.py:466
  87.8 6.2 %grad_one.1 = (f32[8,27,16,128]{3,2,1,0:T(8,128)S(1)}, bf16[4,27,16,128]{3,2,1,0:T(8,128)(2,1)S(1)}, bf16[4,27,16,128]{3,2,1,0:T(8,128)(2,1)S(1)}) custom-call(bf16[1,32,32,128]{3,2,1,0:T(8,128)(2,1)S(1)} %collective-permute-done.1.refs_0_.low, bf16[2,32,32,128]{3,2,1,0:T(8,128)(2,1)S(1)} %copy-done, bf16[2,32,32,128]{3,2,1,0:T(8,128)(2,1)S(1)} %copy-done, ...), custom_call_target="tpu_custom_call" | custom-call | tf_op jit(solution)/shard_map/grad_one/pallas_call | solution.py:484
  99.0 6.1 %collective-permute-done.23.came = bf16[2,27,16,128]{3,2,1,0:T(8,128)(2,1)S(1)} collective-permute-done((bf16[2,27,16,128]{3,2,1,0:T(8,128)(2,1)S(1)}, bf16[2,27,16,128]{3,2,1,0:T(8,128)(2,1)S(1)}, u32[]{:S(2)}, u32[]{:S(2)}) %collective-permute-start.23) | collective-permute-done | bytes 221216 | tf_op jit(solution)/shard_map/ppermute | solution.py:526
  106.0 6.8 %collective-permute-done.24.came = bf16[4,27,16,128]{3,2,1,0:T(8,128)(2,1)S(1)} collective-permute-done((bf16[4,27,16,128]{3,2,1,0:T(8,128)(2,1)S(1)}, bf16[4,27,16,128]{3,2,1,0:T(8,128)(2,1)S(1)}, u32[]{:S(2)}, u32[]{:S(2)}) %collective-permute-start.24) | collective-permute-done | bytes 442400 | tf_op jit(solution)/shard_map/ppermute | solution.py:526
  114.7 4.4 %collective-permute-start.31 = (bf16[1,32,32,256]{3,2,1,0:T(8,128)(2,1)S(1)}, bf16[1,32,32,256]{3,2,1,0:T(8,128)(2,1)S(1)}, u32[]{:S(2)}, u32[]{:S(2)}) collective-permute-start(bf16[1,32,32,256]{3,2,1,0:T(8,128)(2,1)S(1)} %get-tuple-element.113.delta_0.refs_1_), channel_id=1, source_target_pairs={{1,0},{2,1},{3,2},{4,3},{5,4},{6,5},{7,6},{8,7},{9,8},{10,9},{11,1... | collective-permute-start | bytes 1572872 | tf_op jit(solution)/shard_map/ppermute | solution.py:535
  123.2 7.2 %collective-permute-done.29.came = bf16[1,27,16,128]{3,2,1,0:T(8,128)(2,1)S(1)} collective-permute-done((bf16[1,27,16,128]{3,2,1,0:T(8,128)(2,1)S(1)}, bf16[1,27,16,128]{3,2,1,0:T(8,128)(2,1)S(1)}, u32[]{:S(2)}, u32[]{:S(2)}) %collective-permute-start.29) | collective-permute-done | bytes 110624 | tf_op jit(solution)/shard_map/ppermute | solution.py:532
  130.5 3.2 %collective-permute-done.30.came = bf16[2,27,16,128]{3,2,1,0:T(8,128)(2,1)S(1)} collective-permute-done((bf16[2,27,16,128]{3,2,1,0:T(8,128)(2,1)S(1)}, bf16[2,27,16,128]{3,2,1,0:T(8,128)(2,1)S(1)}, u32[]{:S(2)}, u32[]{:S(2)}) %collective-permute-start.30) | collective-permute-done | bytes 221216 | tf_op jit(solution)/shard_map/ppermute | solution.py:529
  134.7 7.2 %collective-permute-done.32.came = bf16[1,27,16,128]{3,2,1,0:T(8,128)(2,1)S(1)} collective-permute-done((bf16[1,27,16,128]{3,2,1,0:T(8,128)(2,1)S(1)}, bf16[1,27,16,128]{3,2,1,0:T(8,128)(2,1)S(1)}, u32[]{:S(2)}, u32[]{:S(2)}) %collective-permute-start.32) | collective-permute-done | bytes 110624 | tf_op jit(solution)/shard_map/ppermute | solution.py:532
  146.3 6.0 %collective-permute-done.34.came = bf16[2,27,16,128]{3,2,1,0:T(8,128)(2,1)S(1)} collective-permute-done((bf16[2,27,16,128]{3,2,1,0:T(8,128)(2,1)S(1)}, bf16[2,27,16,128]{3,2,1,0:T(8,128)(2,1)S(1)}, u32[]{:S(2)}, u32[]{:S(2)}) %collective-permute-start.34) | collective-permute-done | bytes 221216 | tf_op jit(solution)/shard_map/ppermute | solution.py:529
  156.4 9.2 %first_back.1 = bf16[2,32,32,128]{3,2,1,0:T(8,128)(2,1)} custom-call(bf16[1,32,32,256]{3,2,1,0:T(8,128)(2,1)S(1)} %collective-permute-done.25.refs_0_, bf16[1,32,32,256]{3,2,1,0:T(8,128)(2,1)S(1)} %get-tuple-element.113.delta_0.refs_1_, bf16[1,32,32,256]{3,2,1,0:T(8,128)(2,1)S(1)} %get-tuple-element.98.delta_1.refs_2_, ...), custom_call_target="tpu_custom_call" | custom-call | tf_op jit(solution)/shard_map/first_back/pallas_call | solution.py:466
  (90 shorter events, 39.9 us)
Async XLA Ops:
  1.9 16.3 %collective-permute-start = (bf16[27,32,256]{2,1,0:T(8,128)(2,1)S(1)}, bf16[27,32,256]{2,1,0:T(8,128)(2,1)}, u32[]{:S(2)}, u32[]{:S(2)}) collective-permute-start(bf16[27,32,256]{2,1,0:T(8,128)(2,1)S(1)} %constant_dynamic-slice_fusion.1), channel_id=1, source_target_pairs={{0,16},{16,0},{1,17},{17,1},{2,18},{18,2},{3,19},{19,3},{4,20},{20... | collective-permute-start | bytes 1327112 | tf_op jit(solution)/shard_map/ppermute | solution.py:520
  18.2 11.4 %collective-permute-start.3 = (bf16[2,32,32,128]{3,2,1,0:T(8,128)(2,1)S(1)}, bf16[2,32,32,128]{3,2,1,0:T(8,128)(2,1)S(1)}, u32[]{:S(2)}, u32[]{:S(2)}) collective-permute-start(bf16[2,32,32,128]{3,2,1,0:T(8,128)(2,1)S(1)} %copy-done), channel_id=1, source_target_pairs={{0,16},{16,0},{1,17},{17,1},{2,18},{18,2},{3,19},{19,3},{4,20},{20... | collective-permute-start | bytes 1572872 | tf_op jit(solution)/shard_map/ppermute | solution.py:520
  18.7 12.0 %collective-permute-start.6 = (bf16[27,32,256]{2,1,0:T(8,128)(2,1)}, bf16[27,32,256]{2,1,0:T(8,128)(2,1)}, u32[]{:S(2)}, u32[]{:S(2)}) collective-permute-start(bf16[27,32,256]{2,1,0:T(8,128)(2,1)} %collective-permute-done.refs_1_), channel_id=1, source_target_pairs={{0,2},{1,3},{2,0},{3,1},{4,6},{5,7},{6,4},{7,5},{8,10},{9,11},{10,... | collective-permute-start | bytes 1327112 | tf_op jit(solution)/shard_map/ppermute | solution.py:526
  29.6 10.3 %collective-permute-start.9 = (bf16[27,32,256]{2,1,0:T(8,128)(2,1)S(1)}, bf16[27,32,256]{2,1,0:T(8,128)(2,1)S(1)}, u32[]{:S(2)}, u32[]{:S(2)}) collective-permute-start(bf16[27,32,256]{2,1,0:T(8,128)(2,1)S(1)} %constant_dynamic-slice_fusion), channel_id=1, source_target_pairs={{0,16},{16,0},{1,17},{17,1},{2,18},{18,2},{3,19},{19,3},{4,20},{20... | collective-permute-start | bytes 1327112 | tf_op jit(solution)/shard_map/ppermute | solution.py:520
  30.7 10.5 %collective-permute-start.7 = (bf16[27,32,256]{2,1,0:T(8,128)(2,1)}, bf16[27,32,256]{2,1,0:T(8,128)(2,1)S(1)}, u32[]{:S(2)}, u32[]{:S(2)}) collective-permute-start(bf16[27,32,256]{2,1,0:T(8,128)(2,1)} %collective-permute-done.refs_1_), channel_id=1, source_target_pairs={{0,1},{1,0},{2,3},{3,2},{4,5},{5,4},{6,7},{7,6},{8,9},{9,8},{10,11... | collective-permute-start | bytes 1327112 | tf_op jit(solution)/shard_map/ppermute | solution.py:523
  30.7 10.5 %collective-permute-start.8 = (bf16[27,32,256]{2,1,0:T(8,128)(2,1)}, bf16[27,32,256]{2,1,0:T(8,128)(2,1)S(1)}, u32[]{:S(2)}, u32[]{:S(2)}) collective-permute-start(bf16[27,32,256]{2,1,0:T(8,128)(2,1)} %collective-permute-done.6.refs_2_), channel_id=1, source_target_pairs={{0,1},{1,0},{2,3},{3,2},{4,5},{5,4},{6,7},{7,6},{8,9},{9,8},{10,11... | collective-permute-start | bytes 1327112 | tf_op jit(solution)/shard_map/ppermute | solution.py:523
  31.3 14.6 %collective-permute-start.5 = (bf16[1,32,32,128]{3,2,1,0:T(8,128)(2,1)S(1)}, bf16[1,32,32,128]{3,2,1,0:T(8,128)(2,1)S(1)}, u32[]{:S(2)}, u32[]{:S(2)}) collective-permute-start(bf16[1,32,32,128]{3,2,1,0:T(8,128)(2,1)S(1)} %get-tuple-element.116), channel_id=1, source_target_pairs={{1,0},{2,1},{3,2},{4,3},{5,4},{6,5},{7,6},{8,7},{9,8},{10,9},{11,1... | collective-permute-start | bytes 786440 | tf_op jit(solution)/shard_map/ppermute | solution.py:535
  34.5 11.4 %collective-permute-start.4 = (bf16[1,32,32,128]{3,2,1,0:T(8,128)(2,1)S(1)}, bf16[1,32,32,128]{3,2,1,0:T(8,128)(2,1)S(1)}, u32[]{:S(2)}, u32[]{:S(2)}) collective-permute-start(bf16[1,32,32,128]{3,2,1,0:T(8,128)(2,1)S(1)} %get-tuple-element.117), channel_id=1, source_target_pairs={{0,1},{1,2},{2,3},{3,4},{4,5},{5,6},{6,7},{7,8},{8,9},{9,10},{10,1... | collective-permute-start | bytes 786440 | tf_op jit(solution)/shard_map/ppermute | solution.py:535
  39.9 13.2 %collective-permute-start.12 = (bf16[27,32,256]{2,1,0:T(8,128)(2,1)S(1)}, bf16[27,32,256]{2,1,0:T(8,128)(2,1)S(1)}, u32[]{:S(2)}, u32[]{:S(2)}) collective-permute-start(bf16[27,32,256]{2,1,0:T(8,128)(2,1)S(1)} %collective-permute-done.9.refs_3_), channel_id=1, source_target_pairs={{0,4},{1,5},{2,6},{3,7},{4,0},{5,1},{6,2},{7,3},{8,12},{9,13},{10,... | collective-permute-start | bytes 1327112 | tf_op jit(solution)/shard_map/ppermute | solution.py:529
  48.3 13.7 %collective-permute-start.10 = (bf16[1,32,32,256]{3,2,1,0:T(8,128)(2,1)S(1)}, bf16[1,32,32,256]{3,2,1,0:T(8,128)(2,1)S(1)}, u32[]{:S(2)}, u32[]{:S(2)}) collective-permute-start(bf16[1,32,32,256]{3,2,1,0:T(8,128)(2,1)S(1)} %get-tuple-element.68.refs_1_.mid_1.refs_5_), channel_id=1, source_target_pairs={{0,1},{1,2},{2,3},{3,4},{4,5},{5,6},{6,7},{7,8},{8,9},{9,10},{10,1... | collective-permute-start | bytes 1572872 | tf_op jit(solution)/shard_map/ppermute | solution.py:535
  48.4 13.7 %collective-permute-start.11 = (bf16[1,32,32,256]{3,2,1,0:T(8,128)(2,1)S(1)}, bf16[1,32,32,256]{3,2,1,0:T(8,128)(2,1)S(1)}, u32[]{:S(2)}, u32[]{:S(2)}) collective-permute-start(bf16[1,32,32,256]{3,2,1,0:T(8,128)(2,1)S(1)} %get-tuple-element.69.refs_0_.mid_0.refs_4_), channel_id=1, source_target_pairs={{1,0},{2,1},{3,2},{4,3},{5,4},{6,5},{7,6},{8,7},{9,8},{10,9},{11,1... | collective-permute-start | bytes 1572872 | tf_op jit(solution)/shard_map/ppermute | solution.py:535
  52.8 10.0 %collective-permute-start.15 = (bf16[2,32,32,128]{3,2,1,0:T(8,128)(2,1)S(1)}, bf16[2,32,32,128]{3,2,1,0:T(8,128)(2,1)S(1)}, u32[]{:S(2)}, u32[]{:S(2)}) collective-permute-start(bf16[2,32,32,128]{3,2,1,0:T(8,128)(2,1)S(1)} %copy-done.3), channel_id=1, source_target_pairs={{0,16},{16,0},{1,17},{17,1},{2,18},{18,2},{3,19},{19,3},{4,20},{20... | collective-permute-start | bytes 1572872 | tf_op jit(solution)/shard_map/ppermute | solution.py:520
  67.0 17.1 %collective-permute-start.16 = (bf16[1,32,32,256]{3,2,1,0:T(8,128)(2,1)S(1)}, bf16[1,32,32,256]{3,2,1,0:T(8,128)(2,1)S(1)}, u32[]{:S(2)}, u32[]{:S(2)}) collective-permute-start(bf16[1,32,32,256]{3,2,1,0:T(8,128)(2,1)S(1)} %get-tuple-element.74.delta_1.refs_1_), channel_id=1, source_target_pairs={{0,1},{1,2},{2,3},{3,4},{4,5},{5,6},{6,7},{7,8},{8,9},{9,10},{10,1... | collective-permute-start | bytes 1572872 | tf_op jit(solution)/shard_map/ppermute | solution.py:535
  67.2 16.9 %collective-permute-start.17 = (bf16[1,32,32,256]{3,2,1,0:T(8,128)(2,1)S(1)}, bf16[1,32,32,256]{3,2,1,0:T(8,128)(2,1)S(1)}, u32[]{:S(2)}, u32[]{:S(2)}) collective-permute-start(bf16[1,32,32,256]{3,2,1,0:T(8,128)(2,1)S(1)} %get-tuple-element.75.delta_0.refs_0_), channel_id=1, source_target_pairs={{1,0},{2,1},{3,2},{4,3},{5,4},{6,5},{7,6},{8,7},{9,8},{10,9},{11,1... | collective-permute-start | bytes 1572872 | tf_op jit(solution)/shard_map/ppermute | solution.py:535
  84.3 12.2 %collective-permute-start.20 = (bf16[4,27,16,128]{3,2,1,0:T(8,128)(2,1)S(1)}, bf16[4,27,16,128]{3,2,1,0:T(8,128)(2,1)S(1)}, u32[]{:S(2)}, u32[]{:S(2)}) collective-permute-start(bf16[4,27,16,128]{3,2,1,0:T(8,128)(2,1)S(1)} %get-tuple-element.86), channel_id=1, source_target_pairs={{0,4},{1,5},{2,6},{3,7},{4,0},{5,1},{6,2},{7,3},{8,12},{9,13},{10,... | collective-permute-start | bytes 1327112 | tf_op jit(solution)/shard_map/ppermute | solution.py:529
  97.0 15.8 %collective-permute-start.24 = (bf16[4,27,16,128]{3,2,1,0:T(8,128)(2,1)S(1)}, bf16[4,27,16,128]{3,2,1,0:T(8,128)(2,1)S(1)}, u32[]{:S(2)}, u32[]{:S(2)}) collective-permute-start(bf16[4,27,16,128]{3,2,1,0:T(8,128)(2,1)S(1)} %get-tuple-element.96), channel_id=1, source_target_pairs={{0,2},{1,3},{2,0},{3,1},{4,6},{5,7},{6,4},{7,5},{8,10},{9,11},{10,... | collective-permute-start | bytes 1327112 | tf_op jit(solution)/shard_map/ppermute | solution.py:526
  105.1 8.7 %collective-permute-start.26 = (bf16[1,27,16,128]{3,2,1,0:T(8,128)(2,1)S(1)}, bf16[1,27,16,128]{3,2,1,0:T(8,128)(2,1)S(1)}, u32[]{:S(2)}, u32[]{:S(2)}) collective-permute-start(bf16[1,27,16,128]{3,2,1,0:T(8,128)(2,1)S(1)} %get-tuple-element.100), channel_id=1, source_target_pairs={{0,8},{1,9},{2,10},{3,11},{4,12},{5,13},{6,14},{7,15},{8,0},{9,1},... | collective-permute-start | bytes 331784 | tf_op jit(solution)/shard_map/ppermute | solution.py:532
  114.7 20.0 %collective-permute-start.25 = (bf16[1,32,32,256]{3,2,1,0:T(8,128)(2,1)S(1)}, bf16[1,32,32,256]{3,2,1,0:T(8,128)(2,1)S(1)}, u32[]{:S(2)}, u32[]{:S(2)}) collective-permute-start(bf16[1,32,32,256]{3,2,1,0:T(8,128)(2,1)S(1)} %get-tuple-element.98.delta_1.refs_2_), channel_id=1, source_target_pairs={{0,1},{1,2},{2,3},{3,4},{4,5},{5,6},{6,7},{7,8},{8,9},{9,10},{10,1... | collective-permute-start | bytes 1572872 | tf_op jit(solution)/shard_map/ppermute | solution.py:535
  114.7 20.0 %collective-permute-start.31 = (bf16[1,32,32,256]{3,2,1,0:T(8,128)(2,1)S(1)}, bf16[1,32,32,256]{3,2,1,0:T(8,128)(2,1)S(1)}, u32[]{:S(2)}, u32[]{:S(2)}) collective-permute-start(bf16[1,32,32,256]{3,2,1,0:T(8,128)(2,1)S(1)} %get-tuple-element.113.delta_0.refs_1_), channel_id=1, source_target_pairs={{1,0},{2,1},{3,2},{4,3},{5,4},{6,5},{7,6},{8,7},{9,8},{10,9},{11,1... | collective-permute-start | bytes 1572872 | tf_op jit(solution)/shard_map/ppermute | solution.py:535
  121.0 9.4 %collective-permute-start.29 = (bf16[1,27,16,128]{3,2,1,0:T(8,128)(2,1)S(1)}, bf16[1,27,16,128]{3,2,1,0:T(8,128)(2,1)S(1)}, u32[]{:S(2)}, u32[]{:S(2)}) collective-permute-start(bf16[1,27,16,128]{3,2,1,0:T(8,128)(2,1)S(1)} %get-tuple-element.106), channel_id=1, source_target_pairs={{0,8},{1,9},{2,10},{3,11},{4,12},{5,13},{6,14},{7,15},{8,0},{9,1},... | collective-permute-start | bytes 331784 | tf_op jit(solution)/shard_map/ppermute | solution.py:532
  121.8 11.8 %collective-permute-start.30 = (bf16[2,27,16,128]{3,2,1,0:T(8,128)(2,1)S(1)}, bf16[2,27,16,128]{3,2,1,0:T(8,128)(2,1)S(1)}, u32[]{:S(2)}, u32[]{:S(2)}) collective-permute-start(bf16[2,27,16,128]{3,2,1,0:T(8,128)(2,1)S(1)} %join_two_zz.1.own), channel_id=1, source_target_pairs={{0,4},{1,5},{2,6},{3,7},{4,0},{5,1},{6,2},{7,3},{8,12},{9,13},{10,... | collective-permute-start | bytes 663560 | tf_op jit(solution)/shard_map/ppermute | solution.py:529
  133.7 10.5 %collective-permute-start.33 = (bf16[4,27,16,128]{3,2,1,0:T(8,128)(2,1)S(1)}, bf16[4,27,16,128]{3,2,1,0:T(8,128)(2,1)S(1)}, u32[]{:S(2)}, u32[]{:S(2)}) collective-permute-start(bf16[4,27,16,128]{3,2,1,0:T(8,128)(2,1)S(1)} %join_two_z.1.own), channel_id=1, source_target_pairs={{0,2},{1,3},{2,0},{3,1},{4,6},{5,7},{6,4},{7,5},{8,10},{9,11},{10,... | collective-permute-start | bytes 1327112 | tf_op jit(solution)/shard_map/ppermute | solution.py:526
  144.3 9.9 %collective-permute-start.35 = (bf16[8,27,16,128]{3,2,1,0:T(8,128)(2,1)S(1)}, bf16[8,27,16,128]{3,2,1,0:T(8,128)(2,1)S(1)}, u32[]{:S(2)}, u32[]{:S(2)}) collective-permute-start(bf16[8,27,16,128]{3,2,1,0:T(8,128)(2,1)S(1)} %join_two_x.1.own), channel_id=1, source_target_pairs={{0,1},{1,0},{2,3},{3,2},{4,5},{5,4},{6,7},{7,6},{8,9},{9,8},{10,11... | collective-permute-start | bytes 2654216 | tf_op jit(solution)/shard_map/ppermute | solution.py:523
  152.4 13.2 %collective-permute-start.36 = (bf16[4,27,16,128]{3,2,1,0:T(8,128)(2,1)S(1)}, bf16[4,27,16,128]{3,2,1,0:T(8,128)(2,1)S(1)}, u32[]{:S(2)}, u32[]{:S(2)}) collective-permute-start(bf16[4,27,16,128]{3,2,1,0:T(8,128)(2,1)S(1)} %join_one_z.1.own), channel_id=1, source_target_pairs={{0,2},{1,3},{2,0},{3,1},{4,6},{5,7},{6,4},{7,5},{8,10},{9,11},{10,... | collective-permute-start | bytes 1327112 | tf_op jit(solution)/shard_map/ppermute | solution.py:526
  (18 other events, 149.0 us)

commit v2 on v1

--- a/solution.py
+++ b/solution.py
@@ -13,6 +13,7 @@
 HALF = 128
 FULL = 256
 TILE = 16
+SMALL = 10**9
 VMEM_LIMIT = 32 * 1024 * 1024
 
 
@@ -307,9 +308,11 @@
     outs[0][plane, rows] = value.astype(jnp.bfloat16)
 
 
-def filter_kernel(axis, low, mid_0, mid_1, high, delta_0, delta_1, keep, far, near, turned, moved):
+def filter_kernel(colours, *refs):
+    low, mid_0, mid_1, high, delta_0, delta_1 = refs[:6]
+    outs, (turned, moved) = refs[6:-2], refs[-2:]
     _, _, core = place()
-    bit = place_bits()[axis]
+    bits = place_bits()
     pixels = VOX * VOX
     seam = is_seam()
     sources = ((0, low), (1, mid_0), (2, mid_1), (3, high))
@@ -342,21 +345,26 @@
             moved[2, plane, pl.ds(row + 1, TILE)] = shaped(behind.astype(jnp.bfloat16))
 
     mine = lax.axis_index("chan") == core
-    for b in range(3):
-
-        @pl.loop(0, 3)
-        def _(c):
-            right = moved[c, :, 2 - b : 2 - b + VOX].reshape(2 * pixels, FULL)
-            product = jnp.dot(turned[...], right, preferred_element_type=jnp.float32)
-            kept = jnp.where(mine, product[:, :HALF], product[:, HALF:])
-            sent = jnp.where(mine, product[:, HALF:], product[:, :HALF])
-            for a in range(3):
-                rows = slice(a * HALF, (a + 1) * HALF)
-                tap = a * 9 + b * 3 + c
-                keep[:, tap] = kept[rows].reshape(8, 16, HALF)
+    for tap in range(27):
+        a, b, c = tap // 9, tap // 3 % 3, tap % 3
+        if a:
+            continue
+        right = moved[c, :, 2 - b : 2 - b + VOX].reshape(2 * pixels, FULL)
+        product = jnp.dot(turned[...], right, preferred_element_type=jnp.float32)
+        kept = jnp.where(mine, product[:, :HALF], product[:, HALF:])
+        sent = jnp.where(mine, product[:, HALF:], product[:, :HALF])
+        for a in range(3):
+            rows = slice(a * HALF, (a + 1) * HALF)
+            for at, (first, taps, axis) in enumerate(colours):
+                place_at = a * 9 + b * 3 + c - first
+                if not 0 <= place_at < taps:
+                    continue
+                keep, far, near = outs[3 * at : 3 * at + 3]
+                bit = bits[axis]
+                keep[:, place_at] = kept[rows].reshape(8, 16, HALF)
                 blocks = sent[rows].reshape(2, 4, 16, HALF).astype(far.dtype)
-                far[:, tap] = jnp.where(bit == 0, blocks[1], blocks[0])
-                near[:, tap] = jnp.where(bit == 0, blocks[0], blocks[1])
+                far[:, place_at] = jnp.where(bit == 0, blocks[1], blocks[0])
+                near[:, place_at] = jnp.where(bit == 0, blocks[0], blocks[1])
 
 
 def halve_core_kernel(axis, keep, far, near, kept, sent):
@@ -389,17 +397,29 @@
     target[pl.ds((1 - bit) * half, half)] = came[...]
 
 
-def join_core_kernel(order, own, came, grad):
+def join_core_kernel(order, *refs):
     _, _, core = place()
-    for at, block in enumerate(order):
-        rows = slice(block * 16, block * 16 + 16)
-        first = jnp.where(core == 0, own[at], came[at])
-        second = jnp.where(core == 0, came[at], own[at])
-        grad[:, rows, :HALF] = first.astype(jnp.float32)
-        grad[:, rows, HALF:] = second.astype(jnp.float32)
-
-
-WEIGHT = {"sum_two_core": 0, "first_rim": 3 * 10**9}
+    grad = refs[-1]
+    first_tap = 0
+    for own, came in zip(refs[0:-1:2], refs[1:-1:2]):
+        taps = slice(first_tap, first_tap + own.shape[1])
+        first_tap += own.shape[1]
+        for at, block in enumerate(order):
+            rows = slice(block * 16, block * 16 + 16)
+            first = jnp.where(core == 0, own[at], came[at])
+            second = jnp.where(core == 0, came[at], own[at])
+            grad[taps, rows, :HALF] = first.astype(jnp.float32)
+            grad[taps, rows, HALF:] = second.astype(jnp.float32)
+
+
+WEIGHT = {
+    "sum_two_core": 0,
+    "first_rim": 3 * 10**9,
+    "join_a_zz": 4 * 10**9,
+    "join_b_zz": 4 * 10**9,
+    "join_a_z": 6 * 10**9,
+    "join_b_x": 6 * 10**9,
+}
 
 
 def hint(flops):
@@ -413,38 +433,36 @@
         in_specs=[pl.BlockSpec(memory_space=pltpu.VMEM)] * len(operands),
         out_specs=[pl.BlockSpec(memory_space=pltpu.VMEM)] * len(outs),
         compiler_params=pltpu.CompilerParams(vmem_limit_bytes=VMEM_LIMIT),
-        cost_estimate=hint(WEIGHT.get(name, 3 * 10**9)),
+        cost_estimate=hint(WEIGHT.get(name, SMALL)),
         name=name,
     )(*operands)
 
 
-PART = (27, 16, HALF)
-
-
 def halve_core(axis, keep, far, near, name):
-    outs = [((4,) + PART, jnp.float32), ((4,) + PART, jnp.bfloat16)]
+    outs = [(far.shape, jnp.float32), (far.shape, jnp.bfloat16)]
     return small_call(functools.partial(halve_core_kernel, axis), outs, [keep, far, near], name)
 
 
 def halve(axis, keep, came, name):
-    shape = (keep.shape[0] // 2,) + PART
+    shape = (keep.shape[0] // 2,) + keep.shape[1:]
     outs = [(shape, jnp.float32), (shape, jnp.bfloat16)]
     return small_call(functools.partial(halve_kernel, axis), outs, [keep, came], name)
 
 
 def finish(scale, keep, came, name):
-    outs = [((1,) + PART, jnp.bfloat16)]
+    outs = [(keep.shape, jnp.bfloat16)]
     return small_call(functools.partial(finish_kernel, scale), outs, [keep, came], name)[0]
 
 
 def join(axis, own, came, name):
-    outs = [((2 * own.shape[0],) + PART, jnp.bfloat16)]
+    outs = [((2 * own.shape[0],) + own.shape[1:], jnp.bfloat16)]
     return small_call(functools.partial(join_kernel, axis), outs, [own, came], name)[0]
 
 
-def join_core(order, own, came, name):
+def join_core(order, colours, name):
     outs = [((27, HALF, FULL), jnp.float32)]
-    return small_call(functools.partial(join_core_kernel, order), outs, [own, came], name)[0]
+    operands = [half for pair in colours for half in pair]
+    return small_call(functools.partial(join_core_kernel, order), outs, operands, name)[0]
 
 
 def conv_call(name, part, kind, finish, outs, planes, pieces, begun=(), extra=(), flipped=False):
@@ -475,24 +493,22 @@
     )(*operands)
 
 
-def filter_call(axis, planes, mid_at, deltas, name):
+def filter_call(colours, planes, mid_at, deltas, name):
     narrow = (1, VOX, VOX, HALF)
     specs = [
         pl.BlockSpec(narrow, functools.partial(lambda at, i: (at, 0, 0, 0), at)) for at in mid_at
     ]
     specs += [pl.BlockSpec((1, VOX, VOX, FULL), lambda i: (0, 0, 0, 0))] * 2
-    return pl.pallas_call(
-        functools.partial(filter_kernel, axis),
+    outs = []
+    for _, taps, _ in colours:
+        for blocks, dtype in ((8, jnp.float32), (4, jnp.bfloat16), (4, jnp.bfloat16)):
+            outs.append(jax.ShapeDtypeStruct((blocks, taps, 16, HALF), dtype))
+    values = pl.pallas_call(
+        functools.partial(filter_kernel, colours),
         grid=(1,),
-        out_shape=[
-            jax.ShapeDtypeStruct((8, 27, 16, HALF), jnp.float32),
-            jax.ShapeDtypeStruct((4, 27, 16, HALF), jnp.bfloat16),
-            jax.ShapeDtypeStruct((4, 27, 16, HALF), jnp.bfloat16),
-        ],
+        out_shape=outs,
         in_specs=specs,
-        out_specs=[
-            pl.BlockSpec((size, 27, 16, HALF), lambda i: (0, 0, 0, 0)) for size in (8, 4, 4)
-        ],
+        out_specs=[pl.BlockSpec(out.shape, lambda i: (0, 0, 0, 0)) for out in outs],
         scratch_shapes=[
             pltpu.VMEM((3 * HALF, 2 * VOX * VOX), jnp.bfloat16),
             pltpu.VMEM((3, 2, VOX + 2, VOX, FULL), jnp.bfloat16),
@@ -501,6 +517,7 @@
         cost_estimate=hint(0),
         name=name,
     )(*planes, *deltas)
+    return [values[at : at + 3] for at in range(0, len(values), 3)]
 
 
 def after(value, *earlier):
@@ -537,6 +554,7 @@
     wide = ((1, VOX, VOX, FULL), jnp.bfloat16)
     narrow = ((2, VOX, VOX, HALF), jnp.bfloat16)
     partial = ((2, VOX, VOX, FULL), jnp.float32)
+    half_partial = ((2, VOX, VOX, HALF), jnp.float32)
 
     low_own, high_own = rims(volume[:1], volume[1:])
     one_0 = other(lax.dynamic_slice_in_dim(one, (2 * side + core) * 32, 32, axis=1))
@@ -572,15 +590,17 @@
     two_3 = to_core(two_1)
     pieces = [two, two_0, two_1, two_2, two_3]
     begun, ready = conv_call(
-        "second_local", "local", "both", finish_partial, [partial], [act_0, act_1], pieces
+        "second_local", "local", "both", finish_partial, [partial], [act_0, after(act_1, cot_other)],
+        pieces,
     )
     output, delta_0, delta_1 = conv_call(
         "second_rim", "rim", "ready", finish_second, [narrow, wide, wide], [low_act, high_act],
         [ready], [begun], [cotangent, cot_other],
     )
     low_delta, high_delta = rims(delta_0, delta_1)
-    keep, far, near = filter_call(
-        "z", [low_act, act_0, act_1, high_act], (0, 0, 0, 0), [delta_0, delta_1], "grad_two"
+    ((keep, far, near),) = filter_call(
+        ((0, 27, "z"),), [low_act, act_0, act_1, high_act], (0, 0, 0, 0), [delta_0, delta_1],
+        "grad_two",
     )
     far, near = to_core(far), to_core(near)
     (begun,) = conv_call(
@@ -595,42 +615,64 @@
         "back_rim", "rim", "ready", finish_back, [wide, wide], [after(low_delta, keep_two), high_delta],
         [ready], [begun], [act_0, act_1], flipped=True,
     )
-    keep, far, near = filter_call(
-        "x", [low_own, volume, volume, high_own], (0, 0, 1, 0), [prior_0, prior_1], "grad_one"
-    )
-    far, near = to_core(far), to_core(near)
-    keep_two, sent = halve("x", after(keep_two, keep), came_two, "sum_two_z")
+    (keep_a, *sent_a), (keep_b, *sent_b) = filter_call(
+        ((0, 14, "x"), (14, 13, "z")), [low_own, volume, volume, high_own], (0, 0, 1, 0),
+        [prior_0, prior_1], "grad_one",
+    )
+    sent_a, sent_b = [to_core(half) for half in sent_a], [to_core(half) for half in sent_b]
+    keep_two, sent = halve("x", after(keep_two, keep_a), came_two, "sum_two_z")
     came_two = to_side(sent)
-    keep_one, sent = halve_core("x", after(keep, keep_two), far, near, "sum_one_core")
-    came_one = to_side(sent)
-    keep_two, sent = halve("zz", after(keep_two, keep_one), came_two, "sum_two_x")
+    keep_a, sent = halve_core("x", after(keep_a, keep_two), *sent_a, "sum_a_core")
+    came_a = to_side(sent)
+    keep_b, sent = halve_core("z", after(keep_b, keep_a), *sent_b, "sum_b_core")
+    came_b = to_level(sent)
+    (begun,) = conv_call(
+        "first_back_local", "local", "ready", finish_partial, [half_partial],
+        [after(prior_0, keep_b), prior_1], [own_ready], flipped=True,
+    )
+    keep_two, sent = halve("zz", after(keep_two, begun), came_two, "sum_two_x")
     came_two = to_far_level(sent)
-    keep_one, sent = halve("z", after(keep_one, keep_two), came_one, "sum_one_x")
-    came_one = to_level(sent)
-    low_prior, high_prior = rims(after(prior_0, keep_one), after(prior_1, keep_one))
-    own_two = finish(scale, after(keep_two, keep_one), came_two, "sum_two_zz")
+    keep_a, sent = halve("z", after(keep_a, keep_two), came_a, "sum_a_x")
+    came_a = to_level(sent)
+    keep_b, sent = halve("x", after(keep_b, keep_a), came_b, "sum_b_z")
+    came_b = to_side(sent)
+    low_prior, high_prior = rims(after(prior_0, keep_b), after(prior_1, keep_b))
+    own_two = finish(scale, after(keep_two, keep_b), came_two, "sum_two_zz")
     came_two = to_far_level(own_two)
-    keep_one, sent = halve("zz", after(keep_one, own_two), came_one, "sum_one_z")
-    came_one = to_far_level(sent)
-    own_two = join("zz", after(own_two, keep_one), came_two, "join_two_zz")
+    keep_a, sent = halve("zz", after(keep_a, own_two), came_a, "sum_a_z")
+    came_a = to_far_level(sent)
+    keep_b, sent = halve("zz", after(keep_b, keep_a), came_b, "sum_b_x")
+    came_b = to_far_level(sent)
+    own_two = join("zz", after(own_two, keep_b), came_two, "join_two_zz")
     came_two = to_level(own_two)
-    own_one = finish(scale, after(keep_one, own_two), came_one, "sum_one_zz")
-    came_one = to_far_level(own_one)
-    own_two = join("z", after(own_two, own_one), came_two, "join_two_z")
+    own_a = finish(scale, after(keep_a, own_two), came_a, "sum_a_zz")
+    came_a = to_far_level(own_a)
+    own_b = finish(scale, after(keep_b, own_a), came_b, "sum_b_zz")
+    came_b = to_far_level(own_b)
+    own_two = join("z", after(own_two, own_b), came_two, "join_two_z")
     came_two = to_side(own_two)
-    own_one = join("zz", after(own_one, own_two, low_prior, high_prior), came_one, "join_one_zz")
-    came_one = to_level(own_one)
-    own_two = join("x", after(own_two, own_one), came_two, "join_two_x")
+    own_a = join("zz", after(own_a, own_two, low_prior, high_prior), came_a, "join_a_zz")
+    came_a = to_level(own_a)
+    own_b = join("zz", after(own_b, own_a), came_b, "join_b_zz")
+    came_b = to_side(own_b)
+    own_two = join("x", after(own_two, own_b), came_two, "join_two_x")
     came_two = to_core(own_two)
-    own_one = join("z", after(own_one, own_two), came_one, "join_one_z")
-    came_one = to_side(own_one)
-    summed_two = join_core((0, 1, 4, 5, 2, 3, 6, 7), after(own_two, own_one), came_two, "grads_two")
+    own_a = join("z", after(own_a, own_two), came_a, "join_a_z")
+    came_a = to_side(own_a)
+    own_b = join("x", after(own_b, own_a), came_b, "join_b_x")
+    came_b = to_level(own_b)
     (input_grad,) = conv_call(
-        "first_back", "all", "ready", finish_last, [narrow],
-        [low_prior, after(prior_0, summed_two), prior_1, high_prior], [own_ready], flipped=True,
-    )
-    own_one = join("x", after(own_one, input_grad), came_one, "join_one_x")
-    summed_one = join_core(tuple(range(8)), own_one, to_core(own_one), "grads_one")
+        "first_back_rim", "rim", "ready", finish_last, [narrow],
+        [after(low_prior, own_b), high_prior], [own_ready], [begun], flipped=True,
+    )
+    summed_two = join_core(
+        (0, 1, 4, 5, 2, 3, 6, 7), [(after(own_two, input_grad), came_two)], "grads_two"
+    )
+    own_a = join("x", after(own_a, summed_two), came_a, "join_a_x")
+    came_a = to_core(own_a)
+    own_b = join("z", after(own_b, own_a), came_b, "join_b_z")
+    came_b = to_core(own_b)
+    summed_one = join_core(tuple(range(8)), [(own_a, came_a), (own_b, came_b)], "grads_one")
     shape = filter_one.shape
     return output, input_grad, summed_one.reshape(shape), summed_two.reshape(shape)
 

time: 171 us -> 161 us (0.942)
  waiting for transfers between devices: 66.8 us -> 50.1 us
  starting transfers between devices: 39.8 us -> 48.8 us
  Pallas kernels: 59.4 us -> 57.4 us
    ppermute x5 -> x7, waiting for transfers between devices: 13.1 us -> 3.32 us  [to_level(): return lax.ppermute(values, 'dp', [(i, i ^ 4) for i in range(count)])]
    ppermute x4 -> x6, starting transfers between devices: 2.08 us -> 10.1 us  [to_far_level(): return lax.ppermute(values, 'dp', [(i, i ^ 8) for i in range(count)])]
    ppermute x5 -> x7, waiting for transfers between devices: 15.1 us -> 8.54 us  [to_side(): return lax.ppermute(values, 'dp', [(i, i ^ 2) for i in range(count)])]
    ppermute x5 -> x7, starting transfers between devices: 5.58 us -> 2.63 us  [to_level(): return lax.ppermute(values, 'dp', [(i, i ^ 4) for i in range(count)])]
    pallas_call x2, Pallas kernels: 12.4 us -> 9.55 us  [filter_call(): pl.pallas_call(functools.partial(filter_kernel, colours), grid=(1,), out_...]
    ppermute x5 -> x7, starting transfers between devices: 4.56 us -> 6.82 us  [to_side(): return lax.ppermute(values, 'dp', [(i, i ^ 2) for i in range(count)])]
    ppermute x10 -> x13, starting transfers between devices: 2.31 us -> 3.87 us  [to_core(): return lax.ppermute(values, 'dp', [(i, i ^ 1) for i in range(count)])]
    ppermute x4 -> x6, waiting for transfers between devices: 15.2 us -> 16 us  [to_far_level(): return lax.ppermute(values, 'dp', [(i, i ^ 8) for i in range(count)])]
  transfers between devices with their start and end apart: 38 -> 47, of which waited for: 17 -> 12; matrix products, arithmetic and copies ran while one was open for 1% -> 1% of each run, Pallas kernels for 31% -> 32%
where the time goes in v2:
time: 161 us
  Pallas kernels  57.4 us (36%)
  waiting for transfers between devices  50.1 us (31%)
  starting transfers between devices  48.8 us (30%)
  local copies, waits for them, and re-layouts  3.37 us (2%)
    pallas_call x9, Pallas kernels, conv_call(): pl.pallas_call(functools.partial(conv_kernel, part, kind, flipped, finish...  42.3 us
    ppermute x10, starting transfers between devices, rims(): return (lax.ppermute(last, 'dp', ahead), lax.ppermute(first, 'dp', behind))  20.3 us
    ppermute x6, waiting for transfers between devices, to_far_level(): return lax.ppermute(values, 'dp', [(i, i ^ 8) for i in range(count)])  16 us
    ppermute x6, starting transfers between devices, to_far_level(): return lax.ppermute(values, 'dp', [(i, i ^ 8) for i in range(count)])  10.1 us
    ppermute x4, waiting for transfers between devices, other(): return lax.ppermute(values, 'chan', [(0, 1), (1, 0)])  10 us
    pallas_call x2, Pallas kernels, filter_call(): pl.pallas_call(functools.partial(filter_kernel, colours), grid=(1,), out_...  9.55 us
    ppermute x7, waiting for transfers between devices, to_side(): return lax.ppermute(values, 'dp', [(i, i ^ 2) for i in range(count)])  8.54 us
    ppermute x10, waiting for transfers between devices, rims(): return (lax.ppermute(last, 'dp', ahead), lax.ppermute(first, 'dp', behind))  8.51 us
  transfers between devices with their start and end apart: 47, of which 12 were waited for; matrix products, arithmetic and copies ran while one was open for 1% of the time, Pallas kernels for 32%

profile of v2, /device:TPU:0, one launch (start us, length us, event | category | flops | bytes accessed | tf_op | source)
XLA Modules:
  0.0 160.8 jit_solution(11416400429555641095)
XLA Ops:
  6.0 3.7 %collective-permute-start.2 = (bf16[1,32,32,128]{3,2,1,0:T(8,128)(2,1)S(1)}, bf16[1,32,32,128]{3,2,1,0:T(8,128)(2,1)S(1)}, u32[]{:S(2)}, u32[]{:S(2)}) collective-permute-start(bf16[1,32,32,128]{3,2,1,0:T(8,128)(2,1)S(1)} %get-tuple-element.154), channel_id=1, source_target_pairs={{1,0},{2,1},{3,2},{4,3},{5,4},{6,5},{7,6},{8,7},{9,8},{10,9},{11,1... | collective-permute-start | bytes 786440 | tf_op jit(solution)/shard_map/ppermute | solution.py:552
  9.7 3.9 %collective-permute-done.2.refs_2_.refs_3_ = bf16[1,32,32,128]{3,2,1,0:T(8,128)(2,1)S(1)} collective-permute-done((bf16[1,32,32,128]{3,2,1,0:T(8,128)(2,1)S(1)}, bf16[1,32,32,128]{3,2,1,0:T(8,128)(2,1)S(1)}, u32[]{:S(2)}, u32[]{:S(2)}) %collective-permute-start.2) | collective-permute-done | bytes 262176 | tf_op jit(solution)/shard_map/ppermute | solution.py:552
  13.6 4.6 %collective-permute-done.1.refs_0_ = bf16[1,32,32,128]{3,2,1,0:T(8,128)(2,1)S(1)} collective-permute-done((bf16[1,32,32,128]{3,2,1,0:T(8,128)(2,1)S(1)}, bf16[1,32,32,128]{3,2,1,0:T(8,128)(2,1)S(1)}, u32[]{:S(2)}, u32[]{:S(2)}) %collective-permute-start.1) | collective-permute-done | bytes 262176 | tf_op jit(solution)/shard_map/ppermute | solution.py:552
  19.8 10.0 %collective-permute-done.3.refs_0_ = bf16[2,32,32,128]{3,2,1,0:T(8,128)(2,1)S(1)} collective-permute-done((bf16[2,32,32,128]{3,2,1,0:T(8,128)(2,1)}, bf16[2,32,32,128]{3,2,1,0:T(8,128)(2,1)S(1)}, u32[]{:S(2)}, u32[]{:S(2)}) %collective-permute-start.3) | collective-permute-done | bytes 524320 | tf_op jit(solution)/shard_map/ppermute | solution.py:537
  31.5 3.2 %collective-permute-start.5 = (bf16[1,32,32,128]{3,2,1,0:T(8,128)(2,1)S(1)}, bf16[1,32,32,128]{3,2,1,0:T(8,128)(2,1)S(1)}, u32[]{:S(2)}, u32[]{:S(2)}) collective-permute-start(bf16[1,32,32,128]{3,2,1,0:T(8,128)(2,1)S(1)} %get-tuple-element.152), channel_id=1, source_target_pairs={{1,0},{2,1},{3,2},{4,3},{5,4},{6,5},{7,6},{8,7},{9,8},{10,9},{11,1... | collective-permute-start | bytes 786440 | tf_op jit(solution)/shard_map/ppermute | solution.py:552
  34.7 5.4 %first_own.1 = (f32[2,32,32,256]{3,2,1,0:T(8,128)S(1)}, bf16[27,128,256]{2,1,0:T(8,128)(2,1)S(1)}) custom-call(bf16[1,32,32,128]{3,2,1,0:T(8,128)(2,1)S(1)} %collective-permute-done.1.refs_0_, bf16[2,32,32,128]{3,2,1,0:T(8,128)(2,1)S(1)} %copy-done, bf16[1,32,32,128]{3,2,1,0:T(8,128)(2,1)S(1)} %collective-permute-done.2.refs_2_.refs_3_, ...), custom_call_target="tpu_custom_call" | custom-call | tf_op jit(solution)/shard_map/first_own/pallas_call | solution.py:484
  41.7 4.6 %first_other.1 = (f32[2,32,32,256]{3,2,1,0:T(8,128)S(1)}, bf16[27,128,256]{2,1,0:T(8,128)(2,1)S(1)}) custom-call(bf16[2,32,32,128]{3,2,1,0:T(8,128)(2,1)S(1)} %collective-permute-done.3.refs_0_, bf16[27,32,256]{2,1,0:T(8,128)(2,1)} %collective-permute-done.refs_1_, bf16[27,32,256]{2,1,0:T(8,128)(2,1)} %collective-permute-done.6.refs_2_, ...), custom_call_target="tpu_custom_call" | custom-call | tf_op jit(solution)/shard_map/first_other/pallas_call | solution.py:484
  48.8 4.4 %collective-permute-start.11 = (bf16[1,32,32,256]{3,2,1,0:T(8,128)(2,1)S(1)}, bf16[1,32,32,256]{3,2,1,0:T(8,128)(2,1)S(1)}, u32[]{:S(2)}, u32[]{:S(2)}) collective-permute-start(bf16[1,32,32,256]{3,2,1,0:T(8,128)(2,1)S(1)} %get-tuple-element.87.refs_0_.refs_1_.refs_4_), channel_id=1, source_target_pairs={{1,0},{2,1},{3,2},{4,3},{5,4},{6,5},{7,6},{8,7},{9,8},{10,9},{11,1... | collective-permute-start | bytes 1572872 | tf_op jit(solution)/shard_map/ppermute | solution.py:552
  55.7 6.5 %second_local.1 = (f32[2,32,32,256]{3,2,1,0:T(8,128)S(1)}, bf16[27,256,256]{2,1,0:T(8,128)(2,1)S(1)}) custom-call(bf16[1,32,32,256]{3,2,1,0:T(8,128)(2,1)S(1)} %get-tuple-element.87.refs_0_.refs_1_.refs_4_, bf16[1,32,32,256]{3,2,1,0:T(8,128)(2,1)S(1)} %get-tuple-element.89.refs_1_.refs_2_.refs_5_, bf16[27,128,256]{2,1,0:T(8,128)(2,1)S(1)} %bitcast.5, ...), custom_call_target="tpu_custom_call" | custom-call | tf_op jit(solution)/shard_map/second_local/pallas_call | solution.py:484
  62.2 4.3 %second_rim.1 = (bf16[2,32,32,128]{3,2,1,0:T(8,128)(2,1)}, bf16[1,32,32,256]{3,2,1,0:T(8,128)(2,1)S(1)}, bf16[1,32,32,256]{3,2,1,0:T(8,128)(2,1)S(1)}) custom-call(bf16[1,32,32,256]{3,2,1,0:T(8,128)(2,1)S(1)} %collective-permute-done.10.refs_0_, bf16[1,32,32,256]{3,2,1,0:T(8,128)(2,1)S(1)} %collective-permute-done.11.refs_1_.refs_3_, ...), custom_call_target="tpu_custom_call" | custom-call | tf_op jit(solution)/shard_map/second_rim/pallas_call | solution.py:484
  71.0 4.8 %grad_two.1 = (f32[8,27,16,128]{3,2,1,0:T(8,128)S(1)}, bf16[4,27,16,128]{3,2,1,0:T(8,128)(2,1)S(1)}, bf16[4,27,16,128]{3,2,1,0:T(8,128)(2,1)S(1)}) custom-call(bf16[1,32,32,256]{3,2,1,0:T(8,128)(2,1)S(1)} %collective-permute-done.10.refs_0_, bf16[1,32,32,256]{3,2,1,0:T(8,128)(2,1)S(1)} %get-tuple-element.87.refs_0_.refs_1_.refs_4_, ...), custom_call_target="tpu_custom_call" | custom-call | tf_op jit(solution)/shard_map/grad_two/pallas_call | solution.py:506
  76.3 5.8 %back_local.1.refs_3_ = f32[2,32,32,256]{3,2,1,0:T(8,128)S(1)} custom-call(bf16[1,32,32,256]{3,2,1,0:T(8,128)(2,1)S(1)} %get-tuple-element.94.refs_4_.refs_0_, bf16[1,32,32,256]{3,2,1,0:T(8,128)(2,1)S(1)} %get-tuple-element.93.refs_5_.refs_1_, bf16[27,256,256]{2,1,0:T(8,128)(2,1)S(1)} %get-tuple-element.90.refs_2_), custom_call_target="tpu_custom_call" | custom-call | tf_op jit(solution)/shard_map/back_local/pallas_call | solution.py:484
  82.5 3.4 %back_rim.1 = (bf16[1,32,32,256]{3,2,1,0:T(8,128)(2,1)S(1)}, bf16[1,32,32,256]{3,2,1,0:T(8,128)(2,1)S(1)}) custom-call(bf16[1,32,32,256]{3,2,1,0:T(8,128)(2,1)S(1)} %collective-permute-done.16.refs_0_, bf16[1,32,32,256]{3,2,1,0:T(8,128)(2,1)S(1)} %collective-permute-done.17.refs_1_, bf16[27,256,256]{2,1,0:T(8,128)(2,1)S(1)} %get-tuple-element.90.refs_2_, ...), custom_call_target="tpu_custom_call" | custom-call | tf_op jit(solution)/shard_map/back_rim/pallas_call | solution.py:484
  85.9 4.8 %grad_one.1 = (f32[8,14,16,128]{3,2,1,0:T(8,128)S(1)}, bf16[4,14,16,128]{3,2,1,0:T(8,128)(2,1)S(1)}, bf16[4,14,16,128]{3,2,1,0:T(8,128)(2,1)S(1)}, f32[8,13,16,1...) custom-call(bf16[1,32,32,128]{3,2,1,0:T(8,128)(2,1)S(1)} %collective-permute-done.1.ref, ...), custom_call_target="tpu_custom_call" | custom-call | tf_op jit(solution)/shard_map/grad_one/pallas_call | solution.py:506
  92.2 3.3 %collective-permute-done.20.came = bf16[4,27,16,128]{3,2,1,0:T(8,128)(2,1)S(1)} collective-permute-done((bf16[4,27,16,128]{3,2,1,0:T(8,128)(2,1)S(1)}, bf16[4,27,16,128]{3,2,1,0:T(8,128)(2,1)S(1)}, u32[]{:S(2)}, u32[]{:S(2)}) %collective-permute-start.20) | collective-permute-done | bytes 442400 | tf_op jit(solution)/shard_map/ppermute | solution.py:546
  98.1 5.9 %first_back_local.1.refs_3_ = f32[2,32,32,128]{3,2,1,0:T(8,128)S(1)} custom-call(bf16[1,32,32,256]{3,2,1,0:T(8,128)(2,1)S(1)} %get-tuple-element.142.refs_4_.refs_0_, bf16[1,32,32,256]{3,2,1,0:T(8,128)(2,1)S(1)} %get-tuple-element.127.refs_5_.refs_1_, bf16[27,128,256]{2,1,0:T(8,128)(2,1)S(1)} %get-tuple-element.117.refs_2_), custom_call_target="tpu_custom_call" | custom-call | tf_op jit(solution)/shard_map/first_back_local/pallas_call | solution.py:484
  104.7 3.3 %collective-permute-done.26.came = bf16[4,14,16,128]{3,2,1,0:T(8,128)(2,1)S(1)} collective-permute-done((bf16[4,14,16,128]{3,2,1,0:T(8,128)(2,1)S(1)}, bf16[4,14,16,128]{3,2,1,0:T(8,128)(2,1)S(1)}, u32[]{:S(2)}, u32[]{:S(2)}) %collective-permute-start.26) | collective-permute-done | bytes 229408 | tf_op jit(solution)/shard_map/ppermute | solution.py:543
  108.6 4.4 %collective-permute-start.36 = (bf16[1,32,32,256]{3,2,1,0:T(8,128)(2,1)S(1)}, bf16[1,32,32,256]{3,2,1,0:T(8,128)(2,1)S(1)}, u32[]{:S(2)}, u32[]{:S(2)}) collective-permute-start(bf16[1,32,32,256]{3,2,1,0:T(8,128)(2,1)S(1)} %get-tuple-element.142.refs_4_.refs_0_), channel_id=1, source_target_pairs={{1,0},{2,1},{3,2},{4,3},{5,4},{6,5},{7,6},{8,7},{9,8},{10,9},{11,1... | collective-permute-start | bytes 1572872 | tf_op jit(solution)/shard_map/ppermute | solution.py:552
  113.3 4.1 %collective-permute-start.33 = (bf16[1,14,16,128]{3,2,1,0:T(8,128)(2,1)S(1)}, bf16[1,14,16,128]{3,2,1,0:T(8,128)(2,1)S(1)}, u32[]{:S(2)}, u32[]{:S(2)}) collective-permute-start(bf16[1,14,16,128]{3,2,1,0:T(8,128)(2,1)S(1)} %get-tuple-element.138), channel_id=1, source_target_pairs={{0,8},{1,9},{2,10},{3,11},{4,12},{5,13},{6,14},{7,15},{8,0},{9,1},... | collective-permute-start | bytes 172040 | tf_op jit(solution)/shard_map/ppermute | solution.py:549
  117.3 9.1 %collective-permute-done.32.came = bf16[1,27,16,128]{3,2,1,0:T(8,128)(2,1)S(1)} collective-permute-done((bf16[1,27,16,128]{3,2,1,0:T(8,128)(2,1)S(1)}, bf16[1,27,16,128]{3,2,1,0:T(8,128)(2,1)S(1)}, u32[]{:S(2)}, u32[]{:S(2)}) %collective-permute-start.32) | collective-permute-done | bytes 110624 | tf_op jit(solution)/shard_map/ppermute | solution.py:549
  128.9 3.2 %collective-permute-done.34.came = bf16[1,13,16,128]{3,2,1,0:T(8,128)(2,1)S(1)} collective-permute-done((bf16[1,13,16,128]{3,2,1,0:T(8,128)(2,1)S(1)}, bf16[1,13,16,128]{3,2,1,0:T(8,128)(2,1)S(1)}, u32[]{:S(2)}, u32[]{:S(2)}) %collective-permute-start.34) | collective-permute-done | bytes 53280 | tf_op jit(solution)/shard_map/ppermute | solution.py:549
  136.5 3.7 %collective-permute-done.37.came = bf16[1,14,16,128]{3,2,1,0:T(8,128)(2,1)S(1)} collective-permute-done((bf16[1,14,16,128]{3,2,1,0:T(8,128)(2,1)S(1)}, bf16[1,14,16,128]{3,2,1,0:T(8,128)(2,1)S(1)}, u32[]{:S(2)}, u32[]{:S(2)}) %collective-permute-start.37) | collective-permute-done | bytes 57376 | tf_op jit(solution)/shard_map/ppermute | solution.py:549
  141.6 5.2 %collective-permute-done.39.came = bf16[4,27,16,128]{3,2,1,0:T(8,128)(2,1)S(1)} collective-permute-done((bf16[4,27,16,128]{3,2,1,0:T(8,128)(2,1)S(1)}, bf16[4,27,16,128]{3,2,1,0:T(8,128)(2,1)S(1)}, u32[]{:S(2)}, u32[]{:S(2)}) %collective-permute-start.39) | collective-permute-done | bytes 442400 | tf_op jit(solution)/shard_map/ppermute | solution.py:543
  149.9 4.0 %first_back_rim.1 = bf16[2,32,32,128]{3,2,1,0:T(8,128)(2,1)} custom-call(bf16[1,32,32,256]{3,2,1,0:T(8,128)(2,1)S(1)} %collective-permute-done.28.refs_0_, bf16[1,32,32,256]{3,2,1,0:T(8,128)(2,1)S(1)} %collective-permute-done.36.refs_1_, bf16[27,128,256]{2,1,0:T(8,128)(2,1)S(1)} %get-tuple-element.117.refs_2_, f32[2,32,32,128]{3,2,1,0:T(8,128)S(1)} %first_back_local.1.refs_3_), custom_call_target="tpu_custom_call" | custom-call | tf_op jit(solution)/shard_map/first_back_rim/pallas_call | solution.py:484
  (116 shorter events, 44.1 us)
Async XLA Ops:
  1.9 16.3 %collective-permute-start = (bf16[27,32,256]{2,1,0:T(8,128)(2,1)S(1)}, bf16[27,32,256]{2,1,0:T(8,128)(2,1)}, u32[]{:S(2)}, u32[]{:S(2)}) collective-permute-start(bf16[27,32,256]{2,1,0:T(8,128)(2,1)S(1)} %constant_dynamic-slice_fusion.1), channel_id=1, source_target_pairs={{0,16},{16,0},{1,17},{17,1},{2,18},{18,2},{3,19},{19,3},{4,20},{20... | collective-permute-start | bytes 1327112 | tf_op jit(solution)/shard_map/ppermute | solution.py:537
  18.2 11.6 %collective-permute-start.3 = (bf16[2,32,32,128]{3,2,1,0:T(8,128)(2,1)}, bf16[2,32,32,128]{3,2,1,0:T(8,128)(2,1)S(1)}, u32[]{:S(2)}, u32[]{:S(2)}) collective-permute-start(bf16[2,32,32,128]{3,2,1,0:T(8,128)(2,1)} %refs_2_.1), channel_id=1, source_target_pairs={{0,16},{16,0},{1,17},{17,1},{2,18},{18,2},{3,19},{19,3},{4,20},{20... | collective-permute-start | bytes 1572872 | tf_op jit(solution)/shard_map/ppermute | solution.py:537
  18.7 12.2 %collective-permute-start.6 = (bf16[27,32,256]{2,1,0:T(8,128)(2,1)}, bf16[27,32,256]{2,1,0:T(8,128)(2,1)}, u32[]{:S(2)}, u32[]{:S(2)}) collective-permute-start(bf16[27,32,256]{2,1,0:T(8,128)(2,1)} %collective-permute-done.refs_1_), channel_id=1, source_target_pairs={{0,2},{1,3},{2,0},{3,1},{4,6},{5,7},{6,4},{7,5},{8,10},{9,11},{10,... | collective-permute-start | bytes 1327112 | tf_op jit(solution)/shard_map/ppermute | solution.py:543
  29.8 10.3 %collective-permute-start.9 = (bf16[27,32,256]{2,1,0:T(8,128)(2,1)S(1)}, bf16[27,32,256]{2,1,0:T(8,128)(2,1)S(1)}, u32[]{:S(2)}, u32[]{:S(2)}) collective-permute-start(bf16[27,32,256]{2,1,0:T(8,128)(2,1)S(1)} %constant_dynamic-slice_fusion), channel_id=1, source_target_pairs={{0,16},{16,0},{1,17},{17,1},{2,18},{18,2},{3,19},{19,3},{4,20},{20... | collective-permute-start | bytes 1327112 | tf_op jit(solution)/shard_map/ppermute | solution.py:537
  30.9 10.4 %collective-permute-start.7 = (bf16[27,32,256]{2,1,0:T(8,128)(2,1)}, bf16[27,32,256]{2,1,0:T(8,128)(2,1)S(1)}, u32[]{:S(2)}, u32[]{:S(2)}) collective-permute-start(bf16[27,32,256]{2,1,0:T(8,128)(2,1)} %collective-permute-done.refs_1_), channel_id=1, source_target_pairs={{0,1},{1,0},{2,3},{3,2},{4,5},{5,4},{6,7},{7,6},{8,9},{9,8},{10,11... | collective-permute-start | bytes 1327112 | tf_op jit(solution)/shard_map/ppermute | solution.py:540
  30.9 10.8 %collective-permute-start.8 = (bf16[27,32,256]{2,1,0:T(8,128)(2,1)}, bf16[27,32,256]{2,1,0:T(8,128)(2,1)S(1)}, u32[]{:S(2)}, u32[]{:S(2)}) collective-permute-start(bf16[27,32,256]{2,1,0:T(8,128)(2,1)} %collective-permute-done.6.refs_2_), channel_id=1, source_target_pairs={{0,1},{1,0},{2,3},{3,2},{4,5},{5,4},{6,7},{7,6},{8,9},{9,8},{10,11... | collective-permute-start | bytes 1327112 | tf_op jit(solution)/shard_map/ppermute | solution.py:540
  31.5 14.9 %collective-permute-start.5 = (bf16[1,32,32,128]{3,2,1,0:T(8,128)(2,1)S(1)}, bf16[1,32,32,128]{3,2,1,0:T(8,128)(2,1)S(1)}, u32[]{:S(2)}, u32[]{:S(2)}) collective-permute-start(bf16[1,32,32,128]{3,2,1,0:T(8,128)(2,1)S(1)} %get-tuple-element.152), channel_id=1, source_target_pairs={{1,0},{2,1},{3,2},{4,3},{5,4},{6,5},{7,6},{8,7},{9,8},{10,9},{11,1... | collective-permute-start | bytes 786440 | tf_op jit(solution)/shard_map/ppermute | solution.py:552
  34.7 11.7 %collective-permute-start.4 = (bf16[1,32,32,128]{3,2,1,0:T(8,128)(2,1)S(1)}, bf16[1,32,32,128]{3,2,1,0:T(8,128)(2,1)S(1)}, u32[]{:S(2)}, u32[]{:S(2)}) collective-permute-start(bf16[1,32,32,128]{3,2,1,0:T(8,128)(2,1)S(1)} %get-tuple-element.153), channel_id=1, source_target_pairs={{0,1},{1,2},{2,3},{3,4},{4,5},{5,6},{6,7},{7,8},{8,9},{9,10},{10,1... | collective-permute-start | bytes 786440 | tf_op jit(solution)/shard_map/ppermute | solution.py:552
  40.1 13.2 %collective-permute-start.13 = (bf16[27,32,256]{2,1,0:T(8,128)(2,1)S(1)}, bf16[27,32,256]{2,1,0:T(8,128)(2,1)S(1)}, u32[]{:S(2)}, u32[]{:S(2)}) collective-permute-start(bf16[27,32,256]{2,1,0:T(8,128)(2,1)S(1)} %collective-permute-done.9.refs_3_), channel_id=1, source_target_pairs={{0,4},{1,5},{2,6},{3,7},{4,0},{5,1},{6,2},{7,3},{8,12},{9,13},{10,... | collective-permute-start | bytes 1327112 | tf_op jit(solution)/shard_map/ppermute | solution.py:546
  41.3 12.5 %collective-permute-start.12 = (bf16[2,32,32,128]{3,2,1,0:T(8,128)(2,1)S(1)}, bf16[2,32,32,128]{3,2,1,0:T(8,128)(2,1)S(1)}, u32[]{:S(2)}, u32[]{:S(2)}) collective-permute-start(bf16[2,32,32,128]{3,2,1,0:T(8,128)(2,1)S(1)} %copy-done.3), channel_id=1, source_target_pairs={{0,16},{16,0},{1,17},{17,1},{2,18},{18,2},{3,19},{19,3},{4,20},{20... | collective-permute-start | bytes 1572872 | tf_op jit(solution)/shard_map/ppermute | solution.py:537
  48.8 13.5 %collective-permute-start.10 = (bf16[1,32,32,256]{3,2,1,0:T(8,128)(2,1)S(1)}, bf16[1,32,32,256]{3,2,1,0:T(8,128)(2,1)S(1)}, u32[]{:S(2)}, u32[]{:S(2)}) collective-permute-start(bf16[1,32,32,256]{3,2,1,0:T(8,128)(2,1)S(1)} %get-tuple-element.89.refs_1_.refs_2_.refs_5_), channel_id=1, source_target_pairs={{0,1},{1,2},{2,3},{3,4},{4,5},{5,6},{6,7},{7,8},{8,9},{9,10},{10,1... | collective-permute-start | bytes 1572872 | tf_op jit(solution)/shard_map/ppermute | solution.py:552
  48.8 13.4 %collective-permute-start.11 = (bf16[1,32,32,256]{3,2,1,0:T(8,128)(2,1)S(1)}, bf16[1,32,32,256]{3,2,1,0:T(8,128)(2,1)S(1)}, u32[]{:S(2)}, u32[]{:S(2)}) collective-permute-start(bf16[1,32,32,256]{3,2,1,0:T(8,128)(2,1)S(1)} %get-tuple-element.87.refs_0_.refs_1_.refs_4_), channel_id=1, source_target_pairs={{1,0},{2,1},{3,2},{4,3},{5,4},{6,5},{7,6},{8,7},{9,8},{10,9},{11,1... | collective-permute-start | bytes 1572872 | tf_op jit(solution)/shard_map/ppermute | solution.py:552
  66.5 15.6 %collective-permute-start.16 = (bf16[1,32,32,256]{3,2,1,0:T(8,128)(2,1)S(1)}, bf16[1,32,32,256]{3,2,1,0:T(8,128)(2,1)S(1)}, u32[]{:S(2)}, u32[]{:S(2)}) collective-permute-start(bf16[1,32,32,256]{3,2,1,0:T(8,128)(2,1)S(1)} %get-tuple-element.93.refs_5_.refs_1_), channel_id=1, source_target_pairs={{0,1},{1,2},{2,3},{3,4},{4,5},{5,6},{6,7},{7,8},{8,9},{9,10},{10,1... | collective-permute-start | bytes 1572872 | tf_op jit(solution)/shard_map/ppermute | solution.py:552
  68.9 13.2 %collective-permute-start.17 = (bf16[1,32,32,256]{3,2,1,0:T(8,128)(2,1)S(1)}, bf16[1,32,32,256]{3,2,1,0:T(8,128)(2,1)S(1)}, u32[]{:S(2)}, u32[]{:S(2)}) collective-permute-start(bf16[1,32,32,256]{3,2,1,0:T(8,128)(2,1)S(1)} %get-tuple-element.94.refs_4_.refs_0_), channel_id=1, source_target_pairs={{1,0},{2,1},{3,2},{4,3},{5,4},{6,5},{7,6},{8,7},{9,8},{10,9},{11,1... | collective-permute-start | bytes 1572872 | tf_op jit(solution)/shard_map/ppermute | solution.py:552
  82.4 13.1 %collective-permute-start.20 = (bf16[4,27,16,128]{3,2,1,0:T(8,128)(2,1)S(1)}, bf16[4,27,16,128]{3,2,1,0:T(8,128)(2,1)S(1)}, u32[]{:S(2)}, u32[]{:S(2)}) collective-permute-start(bf16[4,27,16,128]{3,2,1,0:T(8,128)(2,1)S(1)} %get-tuple-element.106), channel_id=1, source_target_pairs={{0,4},{1,5},{2,6},{3,7},{4,0},{5,1},{6,2},{7,3},{8,12},{9,13},{10,... | collective-permute-start | bytes 1327112 | tf_op jit(solution)/shard_map/ppermute | solution.py:546
  95.8 12.2 %collective-permute-start.26 = (bf16[4,14,16,128]{3,2,1,0:T(8,128)(2,1)S(1)}, bf16[4,14,16,128]{3,2,1,0:T(8,128)(2,1)S(1)}, u32[]{:S(2)}, u32[]{:S(2)}) collective-permute-start(bf16[4,14,16,128]{3,2,1,0:T(8,128)(2,1)S(1)} %get-tuple-element.122), channel_id=1, source_target_pairs={{0,2},{1,3},{2,0},{3,1},{4,6},{5,7},{6,4},{7,5},{8,10},{9,11},{10,... | collective-permute-start | bytes 688136 | tf_op jit(solution)/shard_map/ppermute | solution.py:543
  98.0 10.1 %collective-permute-start.27 = (bf16[4,13,16,128]{3,2,1,0:T(8,128)(2,1)S(1)}, bf16[4,13,16,128]{3,2,1,0:T(8,128)(2,1)S(1)}, u32[]{:S(2)}, u32[]{:S(2)}) collective-permute-start(bf16[4,13,16,128]{3,2,1,0:T(8,128)(2,1)S(1)} %get-tuple-element.125), channel_id=1, source_target_pairs={{0,4},{1,5},{2,6},{3,7},{4,0},{5,1},{6,2},{7,3},{8,12},{9,13},{10,... | collective-permute-start | bytes 638984 | tf_op jit(solution)/shard_map/ppermute | solution.py:546
  104.1 8.9 %collective-permute-start.29 = (bf16[1,27,16,128]{3,2,1,0:T(8,128)(2,1)S(1)}, bf16[1,27,16,128]{3,2,1,0:T(8,128)(2,1)S(1)}, u32[]{:S(2)}, u32[]{:S(2)}) collective-permute-start(bf16[1,27,16,128]{3,2,1,0:T(8,128)(2,1)S(1)} %get-tuple-element.129), channel_id=1, source_target_pairs={{0,8},{1,9},{2,10},{3,11},{4,12},{5,13},{6,14},{7,15},{8,0},{9,1},... | collective-permute-start | bytes 331784 | tf_op jit(solution)/shard_map/ppermute | solution.py:549
  108.6 27.9 %collective-permute-start.28 = (bf16[1,32,32,256]{3,2,1,0:T(8,128)(2,1)S(1)}, bf16[1,32,32,256]{3,2,1,0:T(8,128)(2,1)S(1)}, u32[]{:S(2)}, u32[]{:S(2)}) collective-permute-start(bf16[1,32,32,256]{3,2,1,0:T(8,128)(2,1)S(1)} %get-tuple-element.127.refs_5_.refs_1_), channel_id=1, source_target_pairs={{0,1},{1,2},{2,3},{3,4},{4,5},{5,6},{6,7},{7,8},{8,9},{9,10},{10,1... | collective-permute-start | bytes 1572872 | tf_op jit(solution)/shard_map/ppermute | solution.py:552
  108.6 27.9 %collective-permute-start.36 = (bf16[1,32,32,256]{3,2,1,0:T(8,128)(2,1)S(1)}, bf16[1,32,32,256]{3,2,1,0:T(8,128)(2,1)S(1)}, u32[]{:S(2)}, u32[]{:S(2)}) collective-permute-start(bf16[1,32,32,256]{3,2,1,0:T(8,128)(2,1)S(1)} %get-tuple-element.142.refs_4_.refs_0_), channel_id=1, source_target_pairs={{1,0},{2,1},{3,2},{4,3},{5,4},{6,5},{7,6},{8,7},{9,8},{10,9},{11,1... | collective-permute-start | bytes 1572872 | tf_op jit(solution)/shard_map/ppermute | solution.py:552
  113.1 13.3 %collective-permute-start.32 = (bf16[1,27,16,128]{3,2,1,0:T(8,128)(2,1)S(1)}, bf16[1,27,16,128]{3,2,1,0:T(8,128)(2,1)S(1)}, u32[]{:S(2)}, u32[]{:S(2)}) collective-permute-start(bf16[1,27,16,128]{3,2,1,0:T(8,128)(2,1)S(1)} %sum_two_zz.1.own), channel_id=1, source_target_pairs={{0,8},{1,9},{2,10},{3,11},{4,12},{5,13},{6,14},{7,15},{8,0},{9,1},... | collective-permute-start | bytes 331784 | tf_op jit(solution)/shard_map/ppermute | solution.py:549
  113.3 15.6 %collective-permute-start.33 = (bf16[1,14,16,128]{3,2,1,0:T(8,128)(2,1)S(1)}, bf16[1,14,16,128]{3,2,1,0:T(8,128)(2,1)S(1)}, u32[]{:S(2)}, u32[]{:S(2)}) collective-permute-start(bf16[1,14,16,128]{3,2,1,0:T(8,128)(2,1)S(1)} %get-tuple-element.138), channel_id=1, source_target_pairs={{0,8},{1,9},{2,10},{3,11},{4,12},{5,13},{6,14},{7,15},{8,0},{9,1},... | collective-permute-start | bytes 172040 | tf_op jit(solution)/shard_map/ppermute | solution.py:549
  135.1 11.6 %collective-permute-start.39 = (bf16[4,27,16,128]{3,2,1,0:T(8,128)(2,1)S(1)}, bf16[4,27,16,128]{3,2,1,0:T(8,128)(2,1)S(1)}, u32[]{:S(2)}, u32[]{:S(2)}) collective-permute-start(bf16[4,27,16,128]{3,2,1,0:T(8,128)(2,1)S(1)} %join_two_z.1.own), channel_id=1, source_target_pairs={{0,2},{1,3},{2,0},{3,1},{4,6},{5,7},{6,4},{7,5},{8,10},{9,11},{10,... | collective-permute-start | bytes 1327112 | tf_op jit(solution)/shard_map/ppermute | solution.py:543
  147.0 9.1 %collective-permute-start.43 = (bf16[4,14,16,128]{3,2,1,0:T(8,128)(2,1)S(1)}, bf16[4,14,16,128]{3,2,1,0:T(8,128)(2,1)S(1)}, u32[]{:S(2)}, u32[]{:S(2)}) collective-permute-start(bf16[4,14,16,128]{3,2,1,0:T(8,128)(2,1)S(1)} %join_a_z.1.own), channel_id=1, source_target_pairs={{0,2},{1,3},{2,0},{3,1},{4,6},{5,7},{6,4},{7,5},{8,10},{9,11},{10,... | collective-permute-start | bytes 688136 | tf_op jit(solution)/shard_map/ppermute | solution.py:543
  (27 other events, 234.3 us)
